TPU v7x, 32 devices: a whole 2x2x4 slice. The times are simulated.
32 devices in a mesh: dp: 4 (over y, x), space: 8 (over z, core).
Axes of the slice: x: 2, y: 2, z: 4, core: 2. Of those that a mesh axis runs over, the one named last changes fastest.
Arguments:
- images: bfloat16 [4, 64, 64, 1536], P('dp', 'space'), may hold values from -8 to 8
- dw_kernel: bfloat16 [7, 7, 1536], replicated, may hold values from -0.875 to 0.875
- dw_bias: float32 [1536], replicated, may hold values from -3 to 3
- ln_gain: float32 [1536], replicated, may hold values from 0.1 to 1.9
- ln_shift: float32 [1536], replicated, may hold values from -2 to 2
- proj: bfloat16 [1536, 1024], replicated, may hold values from -0.15625 to 0.15625
- text: float32 [4, 1024], P('dp'), may hold values from -6 to 6
- logit_scale: float32 [1], replicated, may hold values from 10 to 100
Outputs:
- loss: float32 [], replicated
- grad_images: bfloat16 [4, 64, 64, 1536], P('dp', 'space')
- kernel_grad: float32 [7, 7, 1536], replicated
- text_grad: float32 [4, 1024], P('dp')
All inputs are finite; a program needn't handle non-finite values.
Results may differ from a plain program's by a relative error of at most 0.0013.
Values may be sent and summed in bfloat16 or wider, within the bound.
A program may use at most 128 MiB of HBM per device.

v0:
```python
import jax
import jax.numpy as jnp
from jax import lax
from jax.sharding import PartitionSpec as P


def with_halo(block, sides, width):
    for axis, dim in sides:
        count = lax.axis_size(axis)
        forward = [(i, i + 1) for i in range(count - 1)]
        backward = [(target, source) for source, target in forward]
        low = lax.ppermute(
            lax.slice_in_dim(block, block.shape[dim] - width, None, axis=dim), axis, forward
        )
        high = lax.ppermute(lax.slice_in_dim(block, 0, width, axis=dim), axis, backward)
        block = jnp.concatenate([low, block, high], axis=dim)
    return block


def normalize(values):
    centre_value = jnp.mean(values, axis=-1, keepdims=True)
    centred = values - centre_value
    spread = jnp.mean(centred * centred, axis=-1, keepdims=True)
    inv_dev = lax.rsqrt(spread + 1e-06)
    return (centred * inv_dev, inv_dev)


def convolve(padded, kernel_float, row_count, col_count):
    result = None
    for a in range(kernel_float.shape[0]):
        for d in range(kernel_float.shape[1]):
            product = padded[:, a : a + row_count, d : d + col_count, :] * kernel_float[a, d]
            result = product if result is None else result + product
    return result


def logsum(scores, axis):
    highest = jnp.max(scores, axis=axis, keepdims=True)
    return jnp.squeeze(highest, axis) + jnp.log(jnp.sum(jnp.exp(scores - highest), axis=axis))


def shards(images, dw_kernel, dw_bias, ln_gain, ln_shift, proj, text, logit_scale):
    batch_dev, row_count, col_count, channels = images.shape
    height = row_count * lax.axis_size("space")
    pixel_count = height * col_count
    reach_rows = dw_kernel.shape[0] // 2
    kernel_float = dw_kernel.astype(jnp.float32)
    extended = with_halo(images, (("space", 1),), reach_rows)
    padded_all = jnp.pad(
        extended.astype(jnp.float32), ((0, 0), (0, 0), (reach_rows, reach_rows), (0, 0))
    )
    conv_out = convolve(padded_all, kernel_float, row_count, col_count) + dw_bias
    normed, inv_dev = normalize(conv_out)
    pool_part = jnp.sum(normed * ln_gain + ln_shift, axis=(1, 2))
    proj_float = proj.astype(jnp.float32)
    pooled = lax.psum(pool_part, "space") / pixel_count
    embedded = jnp.dot(pooled, proj_float, precision=lax.Precision.HIGHEST)
    emb_norm = jnp.sqrt(jnp.sum(embedded * embedded, axis=-1, keepdims=True))
    unit_img = embedded / emb_norm
    text_norm = jnp.sqrt(jnp.sum(text * text, axis=-1, keepdims=True))
    unit_txt = text / text_norm
    all_img, all_txt = (
        lax.all_gather(unit_img, "dp", axis=0, tiled=True),
        lax.all_gather(unit_txt, "dp", axis=0, tiled=True),
    )
    factor = logit_scale[0]
    row_scores = factor * jnp.dot(unit_img, all_txt.T, precision=lax.Precision.HIGHEST)
    col_scores = factor * jnp.dot(all_img, unit_txt.T, precision=lax.Precision.HIGHEST)
    row_logsum = logsum(row_scores, 1)
    col_logsum = logsum(col_scores, 0)
    batch_count = all_img.shape[0]
    owned = lax.axis_index("dp") * batch_dev + jnp.arange(batch_dev, dtype=jnp.int32)
    identity_rows = (jnp.arange(batch_count, dtype=jnp.int32)[None, :] == owned[:, None]).astype(
        jnp.float32
    )
    diagonal = jnp.sum(row_scores * identity_rows, axis=1)
    all_row_logsum, all_col_logsum = (
        lax.all_gather(row_logsum, "dp", axis=0, tiled=True),
        lax.all_gather(col_logsum, "dp", axis=0, tiled=True),
    )
    local_terms = jnp.sum(row_logsum - diagonal) + jnp.sum(col_logsum - diagonal)
    loss = lax.psum(local_terms, "dp") / (2 * batch_count)
    row_grad = (
        0.5
        * (
            jnp.exp(row_scores - row_logsum[:, None])
            + jnp.exp(row_scores - all_col_logsum[None, :])
        )
        - identity_rows
    )
    col_grad = (
        0.5
        * (
            jnp.exp(col_scores - all_row_logsum[:, None])
            + jnp.exp(col_scores - col_logsum[None, :])
        )
        - identity_rows.T
    )
    unit_img_grad = factor * jnp.dot(row_grad, all_txt, precision=lax.Precision.HIGHEST)
    unit_txt_grad = factor * jnp.dot(col_grad.T, all_img, precision=lax.Precision.HIGHEST)
    text_grad = (
        unit_txt_grad - unit_txt * jnp.sum(unit_txt * unit_txt_grad, axis=-1, keepdims=True)
    ) / text_norm
    emb_grad = (
        unit_img_grad - unit_img * jnp.sum(unit_img * unit_img_grad, axis=-1, keepdims=True)
    ) / emb_norm
    weighted = jnp.dot(emb_grad, proj_float.T, precision=lax.Precision.HIGHEST) * ln_gain
    weight_rows = weighted[:, None, None, :]
    weight_mean = jnp.mean(weighted, axis=-1)[:, None, None, None]
    spread_term = jnp.mean(weight_rows * normed, axis=-1, keepdims=True)
    grad_own = inv_dev * (weight_rows - weight_mean - normed * spread_term)
    grad_wide = with_halo(grad_own, (("space", 1),), reach_rows)
    grad_pad = jnp.pad(grad_wide, ((0, 0), (0, 0), (reach_rows, reach_rows), (0, 0)))
    input_grad = None
    for a in range(kernel_float.shape[0]):
        for d in range(kernel_float.shape[1]):
            start_row = 2 * reach_rows - a
            start_col = 2 * reach_rows - d
            product = (
                kernel_float[a, d]
                * grad_pad[
                    :, start_row : start_row + row_count, start_col : start_col + col_count, :
                ]
            )
            input_grad = product if input_grad is None else input_grad + product
    kernel_part = jnp.stack(
        [
            jnp.stack(
                [
                    jnp.sum(
                        grad_own * padded_all[:, a : a + row_count, d : d + col_count, :],
                        axis=(0, 1, 2),
                    )
                    for d in range(kernel_float.shape[1])
                ]
            )
            for a in range(kernel_float.shape[0])
        ]
    )
    kernel_grad = lax.psum(kernel_part, ("dp", "space")) / pixel_count
    return (loss, input_grad.astype(jnp.bfloat16), kernel_grad, text_grad)


def solution(mesh):
    placed = (P("dp", "space", None, None), P(), P(), P(), P(), P(), P("dp", None), P())
    return jax.shard_map(
        shards,
        mesh=mesh,
        in_specs=placed,
        out_specs=(P(), P("dp", "space", None, None), P(), P("dp", None)),
        check_vma=False,
    )
```

profile of v0, /device:TPU:0, one launch (start us, length us, event | category | flops | bytes accessed | tf_op | source)
XLA Modules:
  0.0 490.2 jit_solution(3004790936997582301)
XLA Ops:
  7.2 2.5 fusion.104
  9.7 3.2 collective-permute-start
  12.9 1.3 collective-permute-start.1
  14.9 1.3 multiply_reduce_fusion.53
  16.9 0.9 convert_element_type.28
  17.8 1.3 dynamic-slice
  19.8 9.0 %all-gather.1 = f32[4,1,1024]{2,1,0:T(1,128)S(1)} all-gather(f32[1,1,1024]{2,1,0:T(1,128)S(1)} %fusion.113), channel_id=1, replica_groups=mesh['dp'=4,'space'=8] {'dp'}, dimensions={0}, use_global_device_ids=true | all-gather | bytes 20480 | tf_op jit(solution)/shard_map/all_gather | solution.py:64
  29.5 0.9 slice_reduce_fusion.48
  30.5 4.5 maximum_convert_fusion
  35.4 72.7 %fusion.102 = (f32[8,64]{1,0:T(8,128)S(1)}, f32[1,8,64,1536]{3,2,1,0:T(8,128)}) fusion(f32[1536]{0:T(1024)S(1)} %copy-done.86, f32[1536]{0:T(1024)S(1)} %get-tuple-element.54, f32[1536]{0:T(1024)S(1)} %get-tuple-element.55, f32[1536]{0:T(1024)S(1)} %get-tuple-element.56, f32[1536]{0:T(1024)S(1)} %get-tuple-element.57, ...), kind=kLoop, calls=%fused_computation.331 | loop fusion | flops 77856256 | bytes 30996480 | tf_op jit(solution)/shard_map/reduce_sum | solution.py:21
  108.2 2.5 multiply_reduce_fusion.50
  111.6 16.4 %psum.21 = f32[1,1536]{1,0:T(1,128)S(1)} all-reduce(f32[1,1536]{1,0:T(1,128)S(1)} %reduce_sum.564), channel_id=1, replica_groups=mesh['dp'=4,'space'=8] {'space'}, use_global_device_ids=true, to_apply=%region_3.4 | all-reduce | flops 1536 | bytes 12288 | tf_op jit(solution)/shard_map/psum | solution.py:56
  128.0 1.3 fusion.67
  130.6 8.1 %all-gather = f32[4096]{0:T(1024)S(1)} all-gather(f32[1024]{0:T(1024)S(1)} %broadcast_divide_fusion.1), channel_id=2, replica_groups=mesh['dp'=4,'space'=8] {'dp'}, dimensions={0}, use_global_device_ids=true | all-gather | bytes 20480 | tf_op jit(solution)/shard_map/all_gather | solution.py:63
  139.5 1.3 fusion.79
  142.9 1.2 exponential_reduce_fusion
  148.2 10.3 %all-reduce.4 = (f32[]{:T(128)}, f32[4]{0:T(128)S(1)}, f32[4]{0:T(128)S(1)}) all-reduce(f32[]{:T(128)} %bitcast.11, f32[4]{0:T(128)S(1)} %dynamic-update-slice, f32[4]{0:T(128)S(1)} %dynamic-update-slice.1), channel_id=1, replica_groups=mesh['dp'=4,'space'=8] {'dp'}, use_global_device_ids=true, to_apply=%region_11.12 | all-reduce | flops 9 | bytes 72 | tf_op jit(solution)/shard_map/psum | solution.py:82
  159.4 1.2 subtract_divide_fusion.1
  160.7 2.5 convolution_reduce_fusion
  165.1 30.2 %multiply_reduce_fusion = (f32[1536]{0:T(1024)S(1)}, f32[1536]{0:T(1024)S(1)}, f32[1536]{0:T(1024)S(1)}, f32[1536]{0:T(1024)S(1)}, f32[1536]{0:T(1024)S(1)}, /*i...) fusion(f32[1,14,64,1536]{3,2,1,0:T(8,128)} %maximum_convert_fus, ...), kind=kLoop, calls=%fused_computation.157 | loop fusion | flops 32216064 | bytes 21356544 | tf_op jit(solution)/shard_map/reduce_sum | solution.py:130
  195.3 22.3 %multiply_reduce_fusion.36 = (f32[1536]{0:T(1024)S(1)}, f32[1536]{0:T(1024)S(1)}, f32[1536]{0:T(1024)S(1)}, f32[1536]{0:T(1024)S(1)}, f32[1536]{0:T(1024)S(1)}, ...) fusion(f32[1,8,64,1536]{3,2,1,0:T(8,128)S(1)} %get-tuple-elemen, ...), kind=kLoop, calls=%fused_computation.193 | loop fusion | flops 20427264 | bytes 15022080 | tf_op jit(solution)/shard_map/reduce_sum | solution.py:130
  217.6 27.4 %multiply_reduce_fusion.1 = (f32[1536]{0:T(1024)S(1)}, f32[1536]{0:T(1024)S(1)}, f32[1536]{0:T(1024)S(1)}, f32[1536]{0:T(1024)S(1)}, f32[1536]{0:T(1024)S(1)}, /...) fusion(f32[1,8,64,1536]{3,2,1,0:T(8,128)S(1)} %get-tuple-elemen, ...), kind=kLoop, calls=%fused_computation.158 | loop fusion | flops 28283904 | bytes 15052800 | tf_op jit(solution)/shard_map/reduce_sum | solution.py:130
  245.1 1.5 fusion.103
  271.9 2.3 collective-permute-start.2
  274.2 1.5 collective-permute-start.3
  280.1 0.9 stack.253
  282.2 1.4 multiply_reduce_fusion.51
  283.6 1.9 subtract_divide_fusion
  285.5 119.2 %all-reduce.7.cloned.1.call-done = f32[7,7,1536]{2,1,0:T(8,128)} async-done(((f32[7,7,1536]{2,1,0:T(8,128)}), f32[7,7,1536]{2,1,0:T(8,128)}) %all-reduce.7.cloned.1.call-update) | async-done | bytes 301072 | tf_op jit(solution)/shard_map/psum | solution.py:140
  404.8 1.7 broadcast_multiply_fusion
  406.9 4.7 select_maximum_fusion
  412.0 70.2 %fusion.59 = bf16[1,8,64,1536]{3,2,1,0:T(8,128)(2,1)} fusion(f32[1,14,70,1536]{3,2,1,0:T(8,128)} %select_maximum_fusion, f32[1,8,64,1536]{3,2,1,0:T(8,128)} %copy-done.1, f32[1,3,64,1536]{3,2,1,0:T(8,128)} %collective-permute-done.2, f32[1,3,64,1536]{3,2,1,0:T(8,128)} %collective-permute-done.3, f32[1536]{0:T(1024)S(1)} %copy-done.64, ...), kind=kLoop, calls=%fused_computation.211 | loop fusion | flops 81788928 | bytes 139499520 | tf_op jit(solution)/shard_map/convert_element_type | solution.py:141
  (265 shorter events, 38.5 us)
Async XLA Ops:
  7.2 120.8 %copy-start = (bf16[1536,1024]{1,0:T(8,128)(2,1)S(1)}, bf16[1536,1024]{1,0:T(8,128)(2,1)}, u32[]{:S(2)}) copy-start(bf16[1536,1024]{1,0:T(8,128)(2,1)} %param.13) | copy-start | bytes 9437188
  7.2 397.6 %all-reduce.7.cloned.1.call-start = ((), (), s32[]{:S(2)}) async-start(), calls=%async_computation | async-start | bytes 688128 | tf_op jit(solution)/shard_map/psum | solution.py:140
  9.7 20.8 %collective-permute-start = (bf16[1,3,64,1536]{3,2,1,0:T(8,128)(2,1)}, bf16[1,3,64,1536]{3,2,1,0:T(8,128)(2,1)}, u32[]{:S(2)}, u32[]{:S(2)}) collective-permute-start(bf16[1,3,64,1536]{3,2,1,0:T(8,128)(2,1)} %get-tuple-element.114), channel_id=1, source_target_pairs={{0,1},{1,2},{2,3},{3,4},{4,5},{5,6},{6,7},{8,9},{9,10},{10,11},{11... | collective-permute-start | bytes 1769480 | tf_op jit(solution)/shard_map/ppermute | solution.py:12
  12.9 17.6 %collective-permute-start.1 = (bf16[1,3,64,1536]{3,2,1,0:T(8,128)(2,1)}, bf16[1,3,64,1536]{3,2,1,0:T(8,128)(2,1)}, u32[]{:S(2)}, u32[]{:S(2)}) collective-permute-start(bf16[1,3,64,1536]{3,2,1,0:T(8,128)(2,1)} %get-tuple-element.115), channel_id=1, source_target_pairs={{1,0},{2,1},{3,2},{4,3},{5,4},{6,5},{7,6},{9,8},{10,9},{11,10},{12... | collective-permute-start | bytes 1769480 | tf_op jit(solution)/shard_map/ppermute | solution.py:15
  28.9 6.1 %copy-start.5 = (f32[1536]{0:T(1024)}, f32[1536]{0:T(1024)S(1)}, u32[]{:S(2)}) copy-start(f32[1536]{0:T(1024)S(1)} %get-tuple-element.93) | copy-start | bytes 18436
  28.9 6.1 %copy-start.7 = (f32[1536]{0:T(1024)}, f32[1536]{0:T(1024)S(1)}, u32[]{:S(2)}) copy-start(f32[1536]{0:T(1024)S(1)} %get-tuple-element.94) | copy-start | bytes 18436
  28.9 6.1 %copy-start.9 = (f32[1536]{0:T(1024)}, f32[1536]{0:T(1024)S(1)}, u32[]{:S(2)}) copy-start(f32[1536]{0:T(1024)S(1)} %get-tuple-element.95) | copy-start | bytes 18436
  29.0 6.1 %copy-start.11 = (f32[1536]{0:T(1024)}, f32[1536]{0:T(1024)S(1)}, u32[]{:S(2)}) copy-start(f32[1536]{0:T(1024)S(1)} %get-tuple-element.96) | copy-start | bytes 18436
  29.0 6.1 %copy-start.13 = (f32[1536]{0:T(1024)}, f32[1536]{0:T(1024)S(1)}, u32[]{:S(2)}) copy-start(f32[1536]{0:T(1024)S(1)} %get-tuple-element.97) | copy-start | bytes 18436
  29.0 6.1 %copy-start.15 = (f32[1536]{0:T(1024)}, f32[1536]{0:T(1024)S(1)}, u32[]{:S(2)}) copy-start(f32[1536]{0:T(1024)S(1)} %get-tuple-element.98) | copy-start | bytes 18436
  29.0 6.1 %copy-start.17 = (f32[1536]{0:T(1024)}, f32[1536]{0:T(1024)S(1)}, u32[]{:S(2)}) copy-start(f32[1536]{0:T(1024)S(1)} %get-tuple-element.99) | copy-start | bytes 18436
  29.0 6.1 %copy-start.19 = (f32[1536]{0:T(1024)}, f32[1536]{0:T(1024)S(1)}, u32[]{:S(2)}) copy-start(f32[1536]{0:T(1024)S(1)} %get-tuple-element.100) | copy-start | bytes 18436
  29.0 6.1 %copy-start.21 = (f32[1536]{0:T(1024)}, f32[1536]{0:T(1024)S(1)}, u32[]{:S(2)}) copy-start(f32[1536]{0:T(1024)S(1)} %get-tuple-element.101) | copy-start | bytes 18436
  29.3 5.8 %copy-start.23 = (f32[1536]{0:T(1024)}, f32[1536]{0:T(1024)S(1)}, u32[]{:S(2)}) copy-start(f32[1536]{0:T(1024)S(1)} %get-tuple-element.72) | copy-start | bytes 18436
  29.3 5.8 %copy-start.25 = (f32[1536]{0:T(1024)}, f32[1536]{0:T(1024)S(1)}, u32[]{:S(2)}) copy-start(f32[1536]{0:T(1024)S(1)} %get-tuple-element.73) | copy-start | bytes 18436
  29.4 5.8 %copy-start.27 = (f32[1536]{0:T(1024)}, f32[1536]{0:T(1024)S(1)}, u32[]{:S(2)}) copy-start(f32[1536]{0:T(1024)S(1)} %get-tuple-element.74) | copy-start | bytes 18436
  29.4 5.8 %copy-start.29 = (f32[1536]{0:T(1024)}, f32[1536]{0:T(1024)S(1)}, u32[]{:S(2)}) copy-start(f32[1536]{0:T(1024)S(1)} %get-tuple-element.75) | copy-start | bytes 18436
  29.4 5.8 %copy-start.31 = (f32[1536]{0:T(1024)}, f32[1536]{0:T(1024)S(1)}, u32[]{:S(2)}) copy-start(f32[1536]{0:T(1024)S(1)} %get-tuple-element.76) | copy-start | bytes 18436
  29.4 5.8 %copy-start.33 = (f32[1536]{0:T(1024)}, f32[1536]{0:T(1024)S(1)}, u32[]{:S(2)}) copy-start(f32[1536]{0:T(1024)S(1)} %get-tuple-element.77) | copy-start | bytes 18436
  29.4 5.8 %copy-start.35 = (f32[1536]{0:T(1024)}, f32[1536]{0:T(1024)S(1)}, u32[]{:S(2)}) copy-start(f32[1536]{0:T(1024)S(1)} %get-tuple-element.78) | copy-start | bytes 18436
  29.4 5.8 %copy-start.37 = (f32[1536]{0:T(1024)}, f32[1536]{0:T(1024)S(1)}, u32[]{:S(2)}) copy-start(f32[1536]{0:T(1024)S(1)} %get-tuple-element.79) | copy-start | bytes 18436
  29.4 5.8 %copy-start.39 = (f32[1536]{0:T(1024)}, f32[1536]{0:T(1024)S(1)}, u32[]{:S(2)}) copy-start(f32[1536]{0:T(1024)S(1)} %get-tuple-element.80) | copy-start | bytes 18436
  29.4 5.8 %copy-start.41 = (f32[1536]{0:T(1024)}, f32[1536]{0:T(1024)S(1)}, u32[]{:S(2)}) copy-start(f32[1536]{0:T(1024)S(1)} %get-tuple-element.81) | copy-start | bytes 18436
  29.4 5.8 %copy-start.43 = (f32[1536]{0:T(1024)}, f32[1536]{0:T(1024)S(1)}, u32[]{:S(2)}) copy-start(f32[1536]{0:T(1024)S(1)} %get-tuple-element.82) | copy-start | bytes 18436
  29.4 5.8 %copy-start.45 = (f32[1536]{0:T(1024)}, f32[1536]{0:T(1024)S(1)}, u32[]{:S(2)}) copy-start(f32[1536]{0:T(1024)S(1)} %get-tuple-element.83) | copy-start | bytes 18436
  29.5 5.8 %copy-start.47 = (f32[1536]{0:T(1024)}, f32[1536]{0:T(1024)S(1)}, u32[]{:S(2)}) copy-start(f32[1536]{0:T(1024)S(1)} %get-tuple-element.84) | copy-start | bytes 18436
  29.5 5.8 %copy-start.49 = (f32[1536]{0:T(1024)}, f32[1536]{0:T(1024)S(1)}, u32[]{:S(2)}) copy-start(f32[1536]{0:T(1024)S(1)} %get-tuple-element.85) | copy-start | bytes 18436
  29.5 5.8 %copy-start.51 = (f32[1536]{0:T(1024)}, f32[1536]{0:T(1024)S(1)}, u32[]{:S(2)}) copy-start(f32[1536]{0:T(1024)S(1)} %get-tuple-element.86) | copy-start | bytes 18436
  111.0 31.2 %copy-start.83 = (f32[1,1024]{1,0:T(1,128)S(1)}, f32[1,1024]{1,0:T(1,128)}, u32[]{:S(2)}) copy-start(f32[1,1024]{1,0:T(1,128)} %param.14) | copy-start | bytes 12292
  195.3 49.7 %copy-start.1 = (f32[1,8,64,1536]{3,2,1,0:T(8,128)}, f32[1,8,64,1536]{3,2,1,0:T(8,128)S(1)}, u32[]{:S(2)}) copy-start(f32[1,8,64,1536]{3,2,1,0:T(8,128)S(1)} %get-tuple-element.107) | copy-start | bytes 9437188
  271.9 135.0 %collective-permute-start.2 = (f32[1,3,64,1536]{3,2,1,0:T(8,128)}, f32[1,3,64,1536]{3,2,1,0:T(8,128)}, u32[]{:S(2)}, u32[]{:S(2)}) collective-permute-start(f32[1,3,64,1536]{3,2,1,0:T(8,128)} %get-tuple-element.112), channel_id=1, source_target_pairs={{0,1},{1,2},{2,3},{3,4},{4,5},{5,6},{6,7},{8,9},{9,10},{10,11},{11... | collective-permute-start | bytes 3538952 | tf_op jit(solution)/shard_map/ppermute | solution.py:12
  274.2 132.7 %collective-permute-start.3 = (f32[1,3,64,1536]{3,2,1,0:T(8,128)}, f32[1,3,64,1536]{3,2,1,0:T(8,128)}, u32[]{:S(2)}, u32[]{:S(2)}) collective-permute-start(f32[1,3,64,1536]{3,2,1,0:T(8,128)} %get-tuple-element.113), channel_id=1, source_target_pairs={{1,0},{2,1},{3,2},{4,3},{5,4},{6,5},{7,6},{9,8},{10,9},{11,10},{12... | collective-permute-start | bytes 3538952 | tf_op jit(solution)/shard_map/ppermute | solution.py:15
  (60 other events, 296.8 us)
Sparse Core Ops, SparseCore 0:
  281.8 122.9 all-reduce.6
where the time goes:
time: 492 us; the launch traced here: 490 us
  other arithmetic  249 us (51%)
  waiting for transfers between devices  119 us (24%)
  blocking collectives  43.7 us (9%)
  local copies, waits for them, and re-layouts  39.9 us (8%)
  between operations  23.8 us (5%)
  starting transfers between devices  8.32 us (2%)
  matrix products  5.79 us (1%)
    psum x1, waiting for transfers between devices, shards(): kernel_grad = lax.psum(kernel_part, ('dp', 'space')) / pixel_count  119 us
    reduce_sum x3, other arithmetic, shards(): jnp.sum(grad_own * padded_all[:, a:a + row_count, d:d + col_count, :], ax...  80 us
    reduce_sum x1, other arithmetic, normalize(): centre_value = jnp.mean(values, axis=-1, keepdims=True)  72.7 us
    convert_element_type x1, other arithmetic, shards(): return (loss, input_grad.astype(jnp.bfloat16), kernel_grad, text_grad)  70.2 us
    another operation x56, local copies, waits for them, and re-layouts, shards(): jnp.stack([jnp.sum(grad_own * padded_all[:, a:a + row_count, d:d + col_co...  30.3 us
    psum x1, blocking collectives, shards(): pooled = lax.psum(pool_part, 'space') / pixel_count  16.4 us
    psum x1, blocking collectives, shards(): loss = lax.psum(local_terms, 'dp') / (2 * batch_count)  10.3 us
  transfers between devices with their start and end apart: 5, of which 1 were waited for; matrix products, arithmetic and copies ran while one was open for 3% of the time, Pallas kernels for 0%

commit v1 on v0

v1 whole, which is shorter than its diff:
```python
import functools

import jax
import jax.numpy as jnp
from jax import lax
from jax.experimental import pallas as pl
from jax.experimental.pallas import tpu as pltpu
from jax.sharding import PartitionSpec as P

LANES = 128
PAD = 8
TILE = 32
VMEM_LIMIT = 50 * 1024 * 1024
MESH = pl.DeviceIdType.MESH


def fill_taps(taps_ref, k_ref):
    for i in range(k_ref.shape[0]):
        taps_ref[i] = jnp.broadcast_to(k_ref[i : i + 1, :], taps_ref.shape[1:])


def fill_padded(pad_ref, low_ref, x_ref, high_ref):
    cols = x_ref.shape[1]
    first = 0
    for part in (low_ref, x_ref, high_ref):
        count = part.shape[0]
        pad_ref[first : first + count, PAD : PAD + cols, :] = part[...].astype(jnp.float32)
        first += count


def clear_edges(pad_ref, cols):
    rows = pad_ref.shape[0]
    zeros = jnp.zeros((rows, PAD, LANES), jnp.float32)
    pad_ref[:, 0:PAD, :] = zeros
    pad_ref[:, PAD + cols : PAD + cols + PAD, :] = zeros


def convolve(pad_ref, taps_ref, side, rows, start, flip):
    reach = side // 2
    acc = [None] * rows
    for r in range(rows + side - 1):
        for d in range(side):
            first = PAD - reach + d + start
            x = pad_ref[r, first : first + TILE, :].reshape(TILE // 8, 8, LANES)
            for a in range(side):
                h = r - a
                if 0 <= h < rows:
                    tap = (side - 1 - a) * side + side - 1 - d if flip else a * side + d
                    product = x * taps_ref[tap][None]
                    acc[h] = product if acc[h] is None else acc[h] + product
    return acc


def forward_kernel(side, low_ref, x_ref, high_ref, k_ref, bias_ref, gain_ref, shift_ref,
                   normed_ref, inv_ref, pool_ref, pad_ref, taps_ref, sums_ref):
    step = pl.program_id(0)
    blocks, rows, cols, _ = normed_ref.shape
    channels = blocks * LANES
    fill_taps(taps_ref, k_ref)
    clear_edges(pad_ref, cols)
    fill_padded(pad_ref, low_ref, x_ref, high_ref)
    for start in range(0, cols, TILE):
        acc = convolve(pad_ref, taps_ref, side, rows, start, False)
        for h in range(rows):
            normed_ref[step, h, start : start + TILE, :] = (
                acc[h].reshape(TILE, LANES) + bias_ref[...]
            )

    @pl.when(step == blocks - 1)
    def _():
        sums_ref[...] = jnp.zeros_like(sums_ref)

        def one_row(h, carry):
            total = normed_ref[0, h]
            for b in range(1, blocks):
                total = total + normed_ref[b, h]
            mu = jnp.sum(total, axis=1, keepdims=True) / channels
            mu = jnp.broadcast_to(mu, (cols, LANES))
            total = None
            for b in range(blocks):
                centred = normed_ref[b, h] - mu
                total = centred * centred if total is None else total + centred * centred
            spread = jnp.sum(total, axis=1, keepdims=True) / channels
            inv = jnp.broadcast_to(lax.rsqrt(spread + 1e-6), (cols, LANES))
            inv_ref[h] = inv
            for b in range(blocks):
                normed = (normed_ref[b, h] - mu) * inv
                normed_ref[b, h] = normed
                sums_ref[b] += jnp.sum(normed.reshape(cols // 8, 8, LANES), axis=0)
            return carry

        lax.fori_loop(0, rows, one_row, 0)
        for b in range(blocks):
            span = slice(b * LANES, (b + 1) * LANES)
            pool_ref[:, span] = (
                jnp.sum(sums_ref[b], axis=0, keepdims=True) * gain_ref[:, span]
                + (rows * cols) * shift_ref[:, span]
            )


def backward_kernel(side, nlow_ref, normed_ref, nhigh_ref, ilow_ref, inv_ref, ihigh_ref,
                    low_ref, x_ref, high_ref, k_ref, weight_ref, centred_ref,
                    grad_ref, taps_grad_ref, pad_ref, gpad_ref, taps_ref, coef_ref):
    step = pl.program_id(0)
    blocks, rows, cols, _ = normed_ref.shape
    channels = blocks * LANES
    reach = side // 2
    parts = (
        (nlow_ref, ilow_ref, 0),
        (normed_ref, inv_ref, reach),
        (nhigh_ref, ihigh_ref, reach + rows),
    )

    @pl.when(step == 0)
    def _():
        clear_edges(pad_ref, cols)
        clear_edges(gpad_ref, cols)
        for n_ref, i_ref, first in parts:
            def one_row(h, carry):
                total = None
                for b in range(blocks):
                    term = n_ref[b, h] * weight_ref[b]
                    total = term if total is None else total + term
                mean = jnp.sum(total, axis=1, keepdims=True) / channels
                coef_ref[first + h] = i_ref[h] * jnp.broadcast_to(mean, (cols, LANES))
                return carry

            lax.fori_loop(0, n_ref.shape[1], one_row, 0)

    fill_taps(taps_ref, k_ref)
    fill_padded(pad_ref, low_ref, x_ref, high_ref)
    for n_ref, i_ref, first in parts:
        for h in range(n_ref.shape[1]):
            gpad_ref[first + h, PAD : PAD + cols, :] = (
                i_ref[h] * centred_ref[step] - n_ref[step, h] * coef_ref[first + h]
            )
    for d in range(side):
        acc = [None] * side
        for w in range(0, cols, 8):
            own = [gpad_ref[reach + h, PAD + w : PAD + w + 8, :] for h in range(rows)]
            for r in range(rows + side - 1):
                x = pad_ref[r, PAD - reach + d + w : PAD - reach + d + w + 8, :]
                for a in range(side):
                    h = r - a
                    if 0 <= h < rows:
                        product = x * own[h]
                        acc[a] = product if acc[a] is None else acc[a] + product
        for a in range(side):
            tap = a * side + d
            taps_grad_ref[tap : tap + 1, :] = jnp.sum(acc[a], axis=0, keepdims=True)
    for start in range(0, cols, TILE):
        acc = convolve(gpad_ref, taps_ref, side, rows, start, True)
        for h in range(rows):
            grad_ref[h, start : start + TILE, :] = acc[h].reshape(TILE, LANES).astype(
                grad_ref.dtype
            )


def entry_barrier(names):
    barrier = pltpu.get_barrier_semaphore()
    count = 0
    for name in names:
        size = lax.axis_size(name)
        me = lax.axis_index(name)
        for j in range(1, size):
            pl.semaphore_signal(
                barrier, inc=1, device_id={name: lax.rem(me + j, size)}, device_id_type=MESH
            )
        count += size - 1
    pl.semaphore_wait(barrier, count)


def exchange(name, source, target, send_sem, recv_sem):
    size = lax.axis_size(name)
    me = lax.axis_index(name)
    copies = []
    for j in range(1, size):
        peer = lax.rem(me + j, size)
        copy = pltpu.make_async_remote_copy(
            src_ref=source(peer),
            dst_ref=target(j),
            send_sem=send_sem.at[j],
            recv_sem=recv_sem.at[j],
            device_id={name: peer},
            device_id_type=MESH,
        )
        copy.start()
        copies.append(copy)
    return copies


def wait_all(copies):
    for copy in copies:
        copy.wait()


def split3(row):
    one = row.astype(jnp.bfloat16)
    rest = row - one.astype(jnp.float32)
    two = rest.astype(jnp.bfloat16)
    three = (rest - two.astype(jnp.float32)).astype(jnp.bfloat16)
    return jnp.concatenate(
        [one, two, three, jnp.zeros((13, row.shape[1]), jnp.bfloat16)], axis=0
    )


def logsum(scores, axis):
    highest = jnp.max(scores, axis=axis, keepdims=True)
    return highest + jnp.log(jnp.sum(jnp.exp(scores - highest), axis=axis, keepdims=True))


def head_kernel(pixel_count, pool_ref, proj_ref, text_ref, gain_ref, scale_ref,
                weight_ref, loss_ref, text_grad_ref,
                pools_ref, txts_ref, imgs_ref, *sems):
    dp, space = lax.axis_size("dp"), lax.axis_size("space")
    me = lax.axis_index("dp")
    entry_barrier(("dp", "space"))
    pool_copies = exchange("space", lambda p: pool_ref, lambda j: pools_ref.at[j], sems[0], sems[1])
    text = text_ref[...]
    text_norm = jnp.sqrt(jnp.sum(text * text, axis=1, keepdims=True))
    unit_txt = text / text_norm
    txts_ref[me] = unit_txt
    txt_copies = exchange(
        "dp", lambda p: txts_ref.at[me], lambda j: txts_ref.at[me], sems[2], sems[3]
    )
    wait_all(pool_copies)
    pools_ref[0] = pool_ref[...]
    mine = lax.axis_index("space")
    pooled = None
    for s in range(space):
        term = pools_ref[lax.rem(mine - s + space, space)]
        pooled = term if pooled is None else pooled + term
    pooled = pooled / pixel_count
    embedded = jnp.sum(
        jnp.dot(split3(pooled), proj_ref[...], preferred_element_type=jnp.float32),
        axis=0, keepdims=True,
    )
    emb_norm = jnp.sqrt(jnp.sum(embedded * embedded, axis=1, keepdims=True))
    unit_img = embedded / emb_norm
    imgs_ref[me] = unit_img
    img_copies = exchange(
        "dp", lambda p: imgs_ref.at[me], lambda j: imgs_ref.at[me], sems[4], sems[5]
    )
    wait_all(txt_copies)
    wait_all(img_copies)
    imgs = jnp.concatenate([imgs_ref[i] for i in range(dp)], axis=0)
    txts = jnp.concatenate([txts_ref[i] for i in range(dp)], axis=0)
    factor = scale_ref[0]
    row_id = lax.broadcasted_iota(jnp.int32, (dp, dp), 0)
    col_id = lax.broadcasted_iota(jnp.int32, (dp, dp), 1)
    scores = jnp.zeros((dp, dp), jnp.float32)
    turned = jnp.zeros((dp, dp), jnp.float32)
    for i in range(dp):
        column = factor * jnp.sum(imgs * txts[i : i + 1], axis=1, keepdims=True)
        scores = jnp.where(col_id == i, column, scores)
        column = factor * jnp.sum(txts * imgs[i : i + 1], axis=1, keepdims=True)
        turned = jnp.where(col_id == i, column, turned)
    identity = (row_id == col_id).astype(jnp.float32)
    row_ls, col_ls = logsum(scores, 1), logsum(scores, 0)
    trow_ls, tcol_ls = logsum(turned, 1), logsum(turned, 0)
    diagonal = jnp.sum(scores * identity, axis=1, keepdims=True)
    tdiagonal = jnp.sum(turned * identity, axis=1, keepdims=True)
    loss = jnp.sum(row_ls - diagonal, axis=0, keepdims=True) + jnp.sum(
        trow_ls - tdiagonal, axis=0, keepdims=True
    )
    loss_ref[...] = loss / (2 * dp)
    grad = 0.5 * (jnp.exp(scores - row_ls) + jnp.exp(scores - col_ls)) - identity
    tgrad = 0.5 * (jnp.exp(turned - trow_ls) + jnp.exp(turned - tcol_ls)) - identity
    own = (col_id == me).astype(jnp.float32)
    own_img = jnp.sum(tgrad * own, axis=1, keepdims=True)
    own_txt = jnp.sum(grad * own, axis=1, keepdims=True)
    unit_img_grad = factor * jnp.sum(own_img * txts, axis=0, keepdims=True)
    unit_txt_grad = factor * jnp.sum(own_txt * imgs, axis=0, keepdims=True)
    text_grad_ref[...] = (
        unit_txt_grad - unit_txt * jnp.sum(unit_txt * unit_txt_grad, axis=1, keepdims=True)
    ) / text_norm
    emb_grad = (
        unit_img_grad - unit_img * jnp.sum(unit_img * unit_img_grad, axis=1, keepdims=True)
    ) / emb_norm
    back = lax.dot_general(
        split3(emb_grad), proj_ref[...], (((1,), (1,)), ((), ())),
        preferred_element_type=jnp.float32,
    )
    weight_ref[...] = jnp.sum(back, axis=0, keepdims=True) * gain_ref[...]


def sum_kernel(part_ref, out_ref, dp_ref, mine_ref, space_ref, *sems):
    dp, space = lax.axis_size("dp"), lax.axis_size("space")
    me_d, me_s = lax.axis_index("dp"), lax.axis_index("space")
    entry_barrier(("dp", "space"))
    wait_all(exchange("dp", lambda p: part_ref.at[p], lambda j: dp_ref.at[j], sems[0], sems[1]))
    total = part_ref[me_d]
    for j in range(1, dp):
        total = total + dp_ref[j]
    mine_ref[...] = total
    wait_all(exchange(
        "space", lambda p: mine_ref.at[p], lambda j: space_ref.at[j], sems[2], sems[3]
    ))
    total = mine_ref[me_s]
    for j in range(1, space):
        total = total + space_ref[j]
    out_ref[me_d, me_s] = total
    wait_all(exchange(
        "space", lambda p: out_ref.at[me_d, me_s], lambda j: out_ref.at[me_d, me_s],
        sems[4], sems[5],
    ))
    wait_all(exchange(
        "dp", lambda p: out_ref.at[me_d], lambda j: out_ref.at[me_d], sems[6], sems[7]
    ))


def neighbours(low_part, high_part):
    count = lax.axis_size("space")
    forward = [(i, i + 1) for i in range(count - 1)]
    backward = [(target, source) for source, target in forward]
    return lax.ppermute(low_part, "space", forward), lax.ppermute(high_part, "space", backward)


def shards(images, dw_kernel, dw_bias, ln_gain, ln_shift, proj, text, logit_scale):
    f32 = jnp.float32
    _, rows, cols, channels = images.shape
    side = dw_kernel.shape[0]
    reach = side // 2
    taps = side * side
    blocks = channels // LANES
    dp, space = lax.axis_size("dp"), lax.axis_size("space")
    pixel_count = rows * space * cols
    vmem = pl.BlockSpec(memory_space=pltpu.VMEM)
    block = images[0]
    low, high = neighbours(block[rows - reach :], block[:reach])
    kernel_rows = dw_kernel.astype(f32).reshape(taps, channels)
    gain = ln_gain.reshape(1, channels)

    def strip(count):
        return pl.BlockSpec((count, cols, LANES), lambda c: (0, 0, c))

    def whole(*shape):
        return pl.BlockSpec(shape, lambda c: (0,) * len(shape))

    lane_row = pl.BlockSpec((1, LANES), lambda c: (0, c))
    tap_rows = pl.BlockSpec((taps, LANES), lambda c: (0, c))
    padded = pltpu.VMEM((rows + 2 * reach, cols + 2 * PAD, LANES), f32)
    normed, inv, pool = pl.pallas_call(
        functools.partial(forward_kernel, side),
        grid=(blocks,),
        in_specs=[strip(reach), strip(rows), strip(reach), tap_rows, lane_row,
                  whole(1, channels), whole(1, channels)],
        out_specs=[whole(blocks, rows, cols, LANES), whole(rows, cols, LANES), whole(1, channels)],
        out_shape=[
            jax.ShapeDtypeStruct((blocks, rows, cols, LANES), f32),
            jax.ShapeDtypeStruct((rows, cols, LANES), f32),
            jax.ShapeDtypeStruct((1, channels), f32),
        ],
        scratch_shapes=[padded, pltpu.VMEM((taps, 8, LANES), f32),
                        pltpu.VMEM((blocks, 8, LANES), f32)],
        compiler_params=pltpu.CompilerParams(vmem_limit_bytes=VMEM_LIMIT),
        name="forward",
    )(low, block, high, kernel_rows, dw_bias.reshape(1, channels), gain,
      ln_shift.reshape(1, channels))
    nlow, nhigh = neighbours(normed[:, rows - reach :], normed[:, :reach])
    ilow, ihigh = neighbours(inv[rows - reach :], inv[:reach])

    embed = proj.shape[1]
    weighted, loss, text_grad = pl.pallas_call(
        functools.partial(head_kernel, pixel_count),
        in_specs=[vmem] * 4 + [pl.BlockSpec(memory_space=pltpu.SMEM)],
        out_specs=[vmem] * 3,
        out_shape=[
            jax.ShapeDtypeStruct((1, channels), f32),
            jax.ShapeDtypeStruct((1, 1), f32),
            jax.ShapeDtypeStruct((1, embed), f32),
        ],
        scratch_shapes=[
            pltpu.VMEM((space, 1, channels), f32),
            pltpu.VMEM((dp, 1, embed), f32),
            pltpu.VMEM((dp, 1, embed), f32),
        ]
        + [pltpu.SemaphoreType.DMA((space,))] * 2
        + [pltpu.SemaphoreType.DMA((dp,))] * 4,
        compiler_params=pltpu.CompilerParams(
            collective_id=0, has_side_effects=True, vmem_limit_bytes=VMEM_LIMIT
        ),
        name="head",
    )(pool, proj, text, gain, logit_scale)
    weight_rows = weighted.reshape(blocks, 1, LANES)
    centred = weight_rows - jnp.mean(weighted)

    grad_images, taps_grad = pl.pallas_call(
        functools.partial(backward_kernel, side),
        grid=(blocks,),
        in_specs=[
            whole(blocks, reach, cols, LANES), whole(blocks, rows, cols, LANES),
            whole(blocks, reach, cols, LANES), whole(reach, cols, LANES),
            whole(rows, cols, LANES), whole(reach, cols, LANES),
            strip(reach), strip(rows), strip(reach), tap_rows,
            whole(blocks, 1, LANES), whole(blocks, 1, LANES),
        ],
        out_specs=[strip(rows), tap_rows],
        out_shape=[
            jax.ShapeDtypeStruct((rows, cols, channels), jnp.bfloat16),
            jax.ShapeDtypeStruct((taps, channels), f32),
        ],
        scratch_shapes=[padded, padded, pltpu.VMEM((taps, 8, LANES), f32),
                        pltpu.VMEM((rows + 2 * reach, cols, LANES), f32)],
        compiler_params=pltpu.CompilerParams(vmem_limit_bytes=VMEM_LIMIT),
        name="backward",
    )(nlow, normed, nhigh, ilow, inv, ihigh, low, block, high, kernel_rows, weight_rows, centred)

    total_rows = taps * blocks
    chunk = -(-total_rows // (dp * space))
    chunk += -chunk % 8
    flat = jnp.pad(taps_grad.reshape(total_rows, LANES),
                   ((0, chunk * dp * space - total_rows), (0, 0)))
    summed = pl.pallas_call(
        sum_kernel,
        in_specs=[vmem],
        out_specs=vmem,
        out_shape=jax.ShapeDtypeStruct((dp, space, chunk, LANES), f32),
        scratch_shapes=[
            pltpu.VMEM((dp, space, chunk, LANES), f32),
            pltpu.VMEM((space, chunk, LANES), f32),
            pltpu.VMEM((space, chunk, LANES), f32),
        ]
        + [pltpu.SemaphoreType.DMA((dp,))] * 2
        + [pltpu.SemaphoreType.DMA((space,))] * 4
        + [pltpu.SemaphoreType.DMA((dp,))] * 2,
        compiler_params=pltpu.CompilerParams(
            collective_id=1, has_side_effects=True, vmem_limit_bytes=VMEM_LIMIT
        ),
        name="kernel_sum",
    )(flat.reshape(dp, space, chunk, LANES))
    kernel_grad = summed.reshape(-1, LANES)[:total_rows].reshape(side, side, channels) / pixel_count
    return loss.reshape(()), grad_images[None], kernel_grad, text_grad


def solution(mesh):
    placed = (P("dp", "space", None, None), P(), P(), P(), P(), P(), P("dp", None), P())
    return jax.shard_map(
        shards,
        mesh=mesh,
        in_specs=placed,
        out_specs=(P(), P("dp", "space", None, None), P(), P("dp", None)),
        check_vma=False,
    )
```

time: 492 us -> 120 us (0.24)
  other arithmetic: 249 us -> 0.64 us
  waiting for transfers between devices: 119 us -> 1.64 us
  Pallas kernels: 0 us -> 84 us
  blocking collectives: 43.7 us -> 0 us
  local copies, waits for them, and re-layouts: 39.9 us -> 7.57 us
  between operations: 23.8 us -> 3.91 us
  starting transfers between devices: 8.32 us -> 22.3 us
  matrix products: 5.79 us -> 0 us
    reduce_sum x14 -> x1, other arithmetic: 163 us -> 0.61 us  [shards(): centred = weight_rows - jnp.mean(weighted)]
    psum x1 -> x0, waiting for transfers between devices: 119 us -> none  [shards(): kernel_grad = lax.psum(kernel_part, ('dp', 'space')) / pixel_count]
    pallas_call x0 -> x4, Pallas kernels: none -> 84 us  [the longest x1 26.8 us: shards(): pl.pallas_call(functools.partial(backward_kernel, side), grid=(blocks,),...]
    convert_element_type x3 -> x0, other arithmetic: 75.7 us -> none  [the longest x1 70.2 us: shards(): return (loss, input_grad.astype(jnp.bfloat16), kernel_grad, text_grad)]
    another operation x59 -> x0, local copies, waits for them, and re-layouts: 30.3 us -> none  [the longest x56 30.3 us: shards(): jnp.stack([jnp.sum(grad_own * padded_all[:, a:a + row_count, d:d + col_co...]
    psum x2 -> x0, blocking collectives: 26.6 us -> none  [the longest x1 16.4 us: shards(): pooled = lax.psum(pool_part, 'space') / pixel_count]
    all_gather x2 -> x0, blocking collectives: 17.1 us -> none  [the longest x1 8.99 us: shards(): lax.all_gather(unit_txt, 'dp', axis=0, tiled=True)]
    ppermute x4 -> x6, starting transfers between devices: 8.29 us -> 22.3 us  [the longest x3 18.5 us: neighbours(): lax.ppermute(low_part, 'space', forward)]
  transfers between devices with their start and end apart: 5 -> 6, of which waited for: 1 -> 1; matrix products, arithmetic and copies ran while one was open for 3% -> 1% of each run, Pallas kernels for 0% -> 15%
where the time goes in v1:
time: 120 us
  Pallas kernels  84 us (70%)
  starting transfers between devices  22.3 us (19%)
  local copies, waits for them, and re-layouts  7.57 us (6%)
  between operations  3.91 us (3%)
  waiting for transfers between devices  1.64 us (1%)
    pallas_call x1, Pallas kernels, shards(): pl.pallas_call(functools.partial(backward_kernel, side), grid=(blocks,),...  26.8 us
    pallas_call x1, Pallas kernels, shards(): pl.pallas_call(sum_kernel, in_specs=[vmem], out_specs=vmem, out_shape=jax...  24.6 us
    ppermute x3, starting transfers between devices, neighbours(): lax.ppermute(low_part, 'space', forward)  18.5 us
    pallas_call x1, Pallas kernels, shards(): pl.pallas_call(functools.partial(head_kernel, pixel_count), in_specs=[vme...  17.7 us
    pallas_call x1, Pallas kernels, shards(): pl.pallas_call(functools.partial(forward_kernel, side), grid=(blocks,), i...  15 us
    ppermute x3, starting transfers between devices, neighbours(): lax.ppermute(high_part, 'space', backward)  3.85 us
    slice x1, local copies, waits for them, and re-layouts, shards(): nlow, nhigh = neighbours(normed[:, rows - reach:], normed[:, :reach])  3.54 us
    slice x1, local copies, waits for them, and re-layouts, shards(): low, high = neighbours(block[rows - reach:], block[:reach])  2.48 us
  transfers between devices with their start and end apart: 6, of which 1 were waited for; matrix products, arithmetic and copies ran while one was open for 1% of the time, Pallas kernels for 15%

profile of v1, /device:TPU:0, one launch (start us, length us, event | category | flops | bytes accessed | tf_op | source)
XLA Modules:
  0.0 120.1 jit_solution(3429774283548100054)
XLA Ops:
  0.6 0.0 copy-start
  0.6 0.0 copy-start.6
  0.7 0.0 copy-start.7
  0.7 0.0 copy-start.8
  0.7 0.0 copy-start.5
  0.7 2.5 %slice_bitcast_fusion = (bf16[3,64,1536]{2,1,0:T(8,128)(2,1)}, bf16[3,64,1536]{2,1,0:T(8,128)(2,1)}) fusion(bf16[1,8,64,1536]{3,2,1,0:T(8,128)(2,1)} %param.8), kind=kLoop, calls=%fused_computation | loop fusion | bytes 2359296 | tf_op jit(solution)/shard_map/slice | solution.py:330
  3.2 1.3 %collective-permute-start.1 = (bf16[3,64,1536]{2,1,0:T(8,128)(2,1)}, bf16[3,64,1536]{2,1,0:T(8,128)(2,1)S(1)}, u32[]{:S(2)}, u32[]{:S(2)}) collective-permute-start(bf16[3,64,1536]{2,1,0:T(8,128)(2,1)} %get-tuple-element.22), channel_id=1, source_target_pairs={{1,0},{2,1},{3,2},{4,3},{5,4},{6,5},{7,6},{9,8},{10,9},{11,10},{12... | collective-permute-start | bytes 1769480 | tf_op jit(solution)/shard_map/ppermute | solution.py:316
  4.5 3.1 %collective-permute-start = (bf16[3,64,1536]{2,1,0:T(8,128)(2,1)}, bf16[3,64,1536]{2,1,0:T(8,128)(2,1)S(1)}, u32[]{:S(2)}, u32[]{:S(2)}) collective-permute-start(bf16[3,64,1536]{2,1,0:T(8,128)(2,1)} %get-tuple-element.23), channel_id=1, source_target_pairs={{0,1},{1,2},{2,3},{3,4},{4,5},{5,6},{6,7},{8,9},{9,10},{10,11},{11... | collective-permute-start | bytes 1769480 | tf_op jit(solution)/shard_map/ppermute | solution.py:316
  7.5 0.0 copy-done.6
  7.6 0.0 copy-done.7
  7.6 0.0 copy-start.2
  7.6 0.0 copy-done.8
  7.6 0.1 reshape.65.k_ref
  7.7 0.0 collective-permute-done.1.high_ref
  7.7 1.6 %collective-permute-done.low_ref = bf16[3,64,1536]{2,1,0:T(8,128)(2,1)S(1)} collective-permute-done((bf16[3,64,1536]{2,1,0:T(8,128)(2,1)}, bf16[3,64,1536]{2,1,0:T(8,128)(2,1)S(1)}, u32[]{:S(2)}, u32[]{:S(2)}) %collective-permute-start) | collective-permute-done | bytes 589856 | tf_op jit(solution)/shard_map/ppermute | solution.py:316
  9.3 0.0 copy-done
  9.3 15.0 %forward.1 = (f32[12,8,64,128]{3,2,1,0:T(8,128)}, f32[8,64,128]{2,1,0:T(8,128)S(1)}, f32[1,1536]{1,0:T(1,128)S(1)}) custom-call(bf16[3,64,1536]{2,1,0:T(8,128)(2,1)S(1)} %collective-permute-done.low_ref, bf16[8,64,1536]{2,1,0:T(8,128)(2,1)S(1)} %bitcast.12, bf16[3,64,1536]{2,1,0:T(8,128)(2,1)S(1)} %collective-permute-done.1.high_ref, ...), custom_call_target="tpu_custom_call" | custom-call | tf_op jit(solution)/shard_map/forward/pallas_call | solution.py:343
  24.3 3.5 %fusion = (f32[12,3,64,128]{3,2,1,0:T(8,128)}, f32[12,3,64,128]{3,2,1,0:T(8,128)}) fusion(f32[12,8,64,128]{3,2,1,0:T(8,128)} %get-tuple-element.14.normed_ref), kind=kLoop, calls=%fused_computation.4 | loop fusion | bytes 4718592 | tf_op jit(solution)/shard_map/slice | solution.py:360
  27.9 1.3 %collective-permute-start.3 = (f32[12,3,64,128]{3,2,1,0:T(8,128)}, f32[12,3,64,128]{3,2,1,0:T(8,128)}, u32[]{:S(2)}, u32[]{:S(2)}) collective-permute-start(f32[12,3,64,128]{3,2,1,0:T(8,128)} %get-tuple-element.20), channel_id=1, source_target_pairs={{1,0},{2,1},{3,2},{4,3},{5,4},{6,5},{7,6},{9,8},{10,9},{11,10},{12... | collective-permute-start | bytes 3538952 | tf_op jit(solution)/shard_map/ppermute | solution.py:316
  29.2 10.6 %collective-permute-start.2 = (f32[12,3,64,128]{3,2,1,0:T(8,128)}, f32[12,3,64,128]{3,2,1,0:T(8,128)S(1)}, u32[]{:S(2)}, u32[]{:S(2)}) collective-permute-start(f32[12,3,64,128]{3,2,1,0:T(8,128)} %get-tuple-element.21), channel_id=1, source_target_pairs={{0,1},{1,2},{2,3},{3,4},{4,5},{5,6},{6,7},{8,9},{9,10},{10,11},{11... | collective-permute-start | bytes 3538952 | tf_op jit(solution)/shard_map/ppermute | solution.py:316
  40.4 1.3 %collective-permute-start.5 = (f32[3,64,128]{2,1,0:T(8,128)S(1)}, f32[3,64,128]{2,1,0:T(8,128)S(1)}, u32[]{:S(2)}, u32[]{:S(2)}) collective-permute-start(f32[3,64,128]{2,1,0:T(8,128)S(1)} %get-tuple-element.24), channel_id=1, source_target_pairs={{1,0},{2,1},{3,2},{4,3},{5,4},{6,5},{7,6},{9,8},{10,9},{11,10},{12... | collective-permute-start | bytes 294920 | tf_op jit(solution)/shard_map/ppermute | solution.py:316
  41.7 4.8 %collective-permute-start.4 = (f32[3,64,128]{2,1,0:T(8,128)S(1)}, f32[3,64,128]{2,1,0:T(8,128)S(1)}, u32[]{:S(2)}, u32[]{:S(2)}) collective-permute-start(f32[3,64,128]{2,1,0:T(8,128)S(1)} %get-tuple-element.25), channel_id=1, source_target_pairs={{0,1},{1,2},{2,3},{3,4},{4,5},{5,6},{6,7},{8,9},{9,10},{10,11},{11... | collective-permute-start | bytes 294920 | tf_op jit(solution)/shard_map/ppermute | solution.py:316
  46.6 17.7 %head.1 = (f32[1,1536]{1,0:T(1,128)S(1)}, f32[1,1]{1,0:T(1,128)}, f32[1,1024]{1,0:T(1,128)S(1)}) custom-call(f32[1,1536]{1,0:T(1,128)S(1)} %get-tuple-element.12.pool_ref, bf16[1536,1024]{1,0:T(8,128)(2,1)S(1)} %copy-done.1, f32[1,1024]{1,0:T(1,128)S(1)} %copy-done.4, f32[1,1536]{1,0:T(1,128)S(1)} %copy-done.3, f32[1]{0:T(128)S(6)} %copy.14.scale_ref), custom_call_target="tpu_custom_call" | custom-call | tf_op jit(solution)/shard_map/head/pallas_call | solution.py:364
  64.2 0.6 reduce_sum.9
  65.5 0.0 collective-permute-done.5.ihigh_ref
  65.5 0.0 collective-permute-done.4.ilow_ref
  65.5 0.0 collective-permute-done.3.nhigh_ref
  65.5 0.0 collective-permute-done.2.nlow_ref
  65.5 26.8 %backward.1 = (bf16[8,64,1536]{2,1,0:T(8,128)(2,1)}, f32[49,1536]{1,0:T(8,128)S(1)}) custom-call(f32[12,3,64,128]{3,2,1,0:T(8,128)S(1)} %collective-permute-done.2.nlow_ref, f32[12,8,64,128]{3,2,1,0:T(8,128)} %get-tuple-element.14.normed_ref, f32[12,3,64,128]{3,2,1,0:T(8,128)} %collective-permute-done.3.nhigh_ref, ...), custom_call_target="tpu_custom_call" | custom-call | tf_op jit(solution)/shard_map/backward/pallas_call | solution.py:388
  92.4 24.6 %kernel_sum.1 = f32[4,8,24,128]{3,2,1,0:T(8,128)S(1)} custom-call(f32[4,8,24,128]{3,2,1,0:T(8,128)S(1)} %bitcast.13), custom_call_target="tpu_custom_call" | custom-call | tf_op jit(solution)/shard_map/kernel_sum/pallas_call | solution.py:414
  117.0 0.8 div.14
  118.3 0.6 copy.16
  (16 shorter events, 0.1 us)
Async XLA Ops:
  0.6 8.7 %copy-start = (bf16[1,8,64,1536]{3,2,1,0:T(8,128)(2,1)S(1)}, bf16[1,8,64,1536]{3,2,1,0:T(8,128)(2,1)}, u32[]{:S(2)}) copy-start(bf16[1,8,64,1536]{3,2,1,0:T(8,128)(2,1)} %param.8) | copy-start | bytes 4718596
  0.6 6.9 %copy-start.6 = (f32[1536]{0:T(1024)S(1)}, f32[1536]{0:T(1024)}, u32[]{:S(2)}) copy-start(f32[1536]{0:T(1024)} %param.11) | copy-start | bytes 18436
  0.7 6.9 %copy-start.7 = (f32[1536]{0:T(1024)S(1)}, f32[1536]{0:T(1024)}, u32[]{:S(2)}) copy-start(f32[1536]{0:T(1024)} %param.10) | copy-start | bytes 18436
  0.7 6.9 %copy-start.8 = (f32[1536]{0:T(1024)S(1)}, f32[1536]{0:T(1024)}, u32[]{:S(2)}) copy-start(f32[1536]{0:T(1024)} %param.12) | copy-start | bytes 18436
  0.7 6.9 %copy-start.5 = (bf16[7,7,1536]{2,1,0:T(8,128)(2,1)S(1)}, bf16[7,7,1536]{2,1,0:T(8,128)(2,1)}, u32[]{:S(2)}) copy-start(bf16[7,7,1536]{2,1,0:T(8,128)(2,1)} %param.9) | copy-start | bytes 451588
  3.2 4.5 %collective-permute-start.1 = (bf16[3,64,1536]{2,1,0:T(8,128)(2,1)}, bf16[3,64,1536]{2,1,0:T(8,128)(2,1)S(1)}, u32[]{:S(2)}, u32[]{:S(2)}) collective-permute-start(bf16[3,64,1536]{2,1,0:T(8,128)(2,1)} %get-tuple-element.22), channel_id=1, source_target_pairs={{1,0},{2,1},{3,2},{4,3},{5,4},{6,5},{7,6},{9,8},{10,9},{11,10},{12... | collective-permute-start | bytes 1769480 | tf_op jit(solution)/shard_map/ppermute | solution.py:316
  4.5 4.9 %collective-permute-start = (bf16[3,64,1536]{2,1,0:T(8,128)(2,1)}, bf16[3,64,1536]{2,1,0:T(8,128)(2,1)S(1)}, u32[]{:S(2)}, u32[]{:S(2)}) collective-permute-start(bf16[3,64,1536]{2,1,0:T(8,128)(2,1)} %get-tuple-element.23), channel_id=1, source_target_pairs={{0,1},{1,2},{2,3},{3,4},{4,5},{5,6},{6,7},{8,9},{9,10},{10,11},{11... | collective-permute-start | bytes 1769480 | tf_op jit(solution)/shard_map/ppermute | solution.py:316
  7.6 16.8 %copy-start.2 = (f32[1,1536]{1,0:T(1,128)}, f32[1,1536]{1,0:T(1,128)S(1)}, u32[]{:S(2)}) copy-start(f32[1,1536]{1,0:T(1,128)S(1)} %reshape.57.gain_ref) | copy-start | bytes 18436
  24.3 22.2 %copy-start.1 = (bf16[1536,1024]{1,0:T(8,128)(2,1)S(1)}, bf16[1536,1024]{1,0:T(8,128)(2,1)}, u32[]{:S(2)}) copy-start(bf16[1536,1024]{1,0:T(8,128)(2,1)} %proj_ref.1) | copy-start | bytes 9437188
  24.3 22.2 %copy-start.3 = (f32[1,1536]{1,0:T(1,128)S(1)}, f32[1,1536]{1,0:T(1,128)}, u32[]{:S(2)}) copy-start(f32[1,1536]{1,0:T(1,128)} %copy-done.2) | copy-start | bytes 18436
  24.3 22.2 %copy-start.4 = (f32[1,1024]{1,0:T(1,128)S(1)}, f32[1,1024]{1,0:T(1,128)}, u32[]{:S(2)}) copy-start(f32[1,1024]{1,0:T(1,128)} %text_ref.1) | copy-start | bytes 12292
  27.9 37.7 %collective-permute-start.3 = (f32[12,3,64,128]{3,2,1,0:T(8,128)}, f32[12,3,64,128]{3,2,1,0:T(8,128)}, u32[]{:S(2)}, u32[]{:S(2)}) collective-permute-start(f32[12,3,64,128]{3,2,1,0:T(8,128)} %get-tuple-element.20), channel_id=1, source_target_pairs={{1,0},{2,1},{3,2},{4,3},{5,4},{6,5},{7,6},{9,8},{10,9},{11,10},{12... | collective-permute-start | bytes 3538952 | tf_op jit(solution)/shard_map/ppermute | solution.py:316
  29.2 36.4 %collective-permute-start.2 = (f32[12,3,64,128]{3,2,1,0:T(8,128)}, f32[12,3,64,128]{3,2,1,0:T(8,128)S(1)}, u32[]{:S(2)}, u32[]{:S(2)}) collective-permute-start(f32[12,3,64,128]{3,2,1,0:T(8,128)} %get-tuple-element.21), channel_id=1, source_target_pairs={{0,1},{1,2},{2,3},{3,4},{4,5},{5,6},{6,7},{8,9},{9,10},{10,11},{11... | collective-permute-start | bytes 3538952 | tf_op jit(solution)/shard_map/ppermute | solution.py:316
  40.4 25.1 %collective-permute-start.5 = (f32[3,64,128]{2,1,0:T(8,128)S(1)}, f32[3,64,128]{2,1,0:T(8,128)S(1)}, u32[]{:S(2)}, u32[]{:S(2)}) collective-permute-start(f32[3,64,128]{2,1,0:T(8,128)S(1)} %get-tuple-element.24), channel_id=1, source_target_pairs={{1,0},{2,1},{3,2},{4,3},{5,4},{6,5},{7,6},{9,8},{10,9},{11,10},{12... | collective-permute-start | bytes 294920 | tf_op jit(solution)/shard_map/ppermute | solution.py:316
  41.7 23.8 %collective-permute-start.4 = (f32[3,64,128]{2,1,0:T(8,128)S(1)}, f32[3,64,128]{2,1,0:T(8,128)S(1)}, u32[]{:S(2)}, u32[]{:S(2)}) collective-permute-start(f32[3,64,128]{2,1,0:T(8,128)S(1)} %get-tuple-element.25), channel_id=1, source_target_pairs={{0,1},{1,2},{2,3},{3,4},{4,5},{5,6},{6,7},{8,9},{9,10},{10,11},{11... | collective-permute-start | bytes 294920 | tf_op jit(solution)/shard_map/ppermute | solution.py:316

commit v2 on v1

v2 whole, which is shorter than its diff:
```python
import functools

import jax
import jax.numpy as jnp
from jax import lax
from jax.experimental import pallas as pl
from jax.experimental.pallas import tpu as pltpu
from jax.sharding import PartitionSpec as P

LANES = 128
PAD = 8
TILE = 32
VMEM_LIMIT = 50 * 1024 * 1024
MESH = pl.DeviceIdType.MESH


def fill_taps(taps_ref, rows):
    for i in range(rows.shape[0]):
        taps_ref[i] = jnp.broadcast_to(rows[i : i + 1, :], taps_ref.shape[1:])


def fill_padded(pad_ref, parts, cols):
    first = 0
    for part in parts:
        pad_ref[first : first + part.shape[0], PAD : PAD + cols, :] = part.astype(jnp.float32)
        first += part.shape[0]


def clear_edges(pad_ref, cols):
    rows = pad_ref.shape[0]
    zeros = jnp.zeros((rows, PAD, LANES), jnp.float32)
    pad_ref[:, 0:PAD, :] = zeros
    pad_ref[:, PAD + cols : PAD + cols + PAD, :] = zeros


def convolve(pad_ref, taps_ref, side, rows, start, flip):
    reach = side // 2
    acc = [None] * rows
    for r in range(rows + side - 1):
        for d in range(side):
            first = PAD - reach + d + start
            x = pad_ref[r, first : first + TILE, :].reshape(TILE // 8, 8, LANES)
            for a in range(side):
                h = r - a
                if 0 <= h < rows:
                    tap = (side - 1 - a) * side + side - 1 - d if flip else a * side + d
                    product = x * taps_ref[tap][None]
                    acc[h] = product if acc[h] is None else acc[h] + product
    return acc


def entry_barrier(names):
    barrier = pltpu.get_barrier_semaphore()
    count = 0
    for name in names:
        size = lax.axis_size(name)
        me = lax.axis_index(name)
        for j in range(1, size):
            pl.semaphore_signal(
                barrier, inc=1, device_id={name: lax.rem(me + j, size)}, device_id_type=MESH
            )
        count += size - 1
    pl.semaphore_wait(barrier, count)


def swap(name, source, target, send_sem, recv_sem):
    size = lax.axis_size(name)
    me = lax.axis_index(name)
    copies = []
    for j in range(1, size):
        peer = lax.rem(me + j, size)
        copies.append(pltpu.make_async_remote_copy(
            src_ref=source(peer),
            dst_ref=target(j),
            send_sem=send_sem.at[j],
            recv_sem=recv_sem.at[j],
            device_id={name: peer},
            device_id_type=MESH,
        ))
    return copies


def start_all(copies):
    for copy in copies:
        copy.start()


def exchange(*args):
    copies = swap(*args)
    start_all(copies)
    return copies


def wait_all(copies):
    for copy in copies:
        copy.wait()


def split3(row):
    one = row.astype(jnp.bfloat16)
    rest = row - one.astype(jnp.float32)
    two = rest.astype(jnp.bfloat16)
    three = (rest - two.astype(jnp.float32)).astype(jnp.bfloat16)
    return jnp.concatenate(
        [one, two, three, jnp.zeros((13, row.shape[1]), jnp.bfloat16)], axis=0
    )


def logsum(scores, axis):
    highest = jnp.max(scores, axis=axis, keepdims=True)
    return highest + jnp.log(jnp.sum(jnp.exp(scores - highest), axis=axis, keepdims=True))


def lanes_of(b):
    return pl.ds(pl.multiple_of(b * LANES, LANES), LANES)


def block_kernel(side, pixel_count,
                 image_ref, k_ref, bias_ref, gain_ref, shift_ref, proj_hbm, text_ref, scale_ref,
                 grad_ref, sum_ref, loss_ref, text_grad_ref,
                 low_ref, high_ref, normed_ref, inv_ref, coef_ref, pad_ref, gpad_ref, taps_ref,
                 pool_ref, weight_ref, centred_ref, proj_ref, pools_ref, txts_ref, imgs_ref,
                 part_ref, dp_ref, mine_ref, space_ref,
                 proj_sem, image_sems, wide_sems, *sems):
    rows, cols, channels = image_ref.shape
    blocks = channels // LANES
    reach = side // 2
    dp, space = lax.axis_size("dp"), lax.axis_size("space")
    me, mine = lax.axis_index("dp"), lax.axis_index("space")
    has_low, has_high = mine > 0, mine < space - 1
    share, owned = part_ref.shape[1], part_ref.shape[2] // space

    proj_copy = pltpu.make_async_copy(proj_hbm, proj_ref, proj_sem)
    proj_copy.start()
    entry_barrier(("dp", "space"))

    def to_high(b):
        return pltpu.make_async_remote_copy(
            src_ref=image_ref.at[rows - reach : rows, :, lanes_of(b)], dst_ref=low_ref.at[b],
            send_sem=image_sems.at[0, b], recv_sem=image_sems.at[1, b],
            device_id={"space": mine + 1}, device_id_type=MESH,
        )

    def to_low(b):
        return pltpu.make_async_remote_copy(
            src_ref=image_ref.at[0:reach, :, lanes_of(b)], dst_ref=high_ref.at[b],
            send_sem=image_sems.at[2, b], recv_sem=image_sems.at[3, b],
            device_id={"space": mine - 1}, device_id_type=MESH,
        )

    def send_image(b, carry):
        @pl.when(has_high)
        def _():
            to_high(b).start()

        @pl.when(has_low)
        def _():
            to_low(b).start()

        return carry

    lax.fori_loop(0, blocks, send_image, 0)

    @pl.when(jnp.logical_not(has_low))
    def _():
        low_ref[...] = jnp.zeros_like(low_ref)
        normed_ref[:, 0:reach] = jnp.zeros((blocks, reach, cols, LANES), jnp.float32)
        inv_ref[0:reach] = jnp.zeros((reach, cols, LANES), jnp.float32)

    @pl.when(jnp.logical_not(has_high))
    def _():
        high_ref[...] = jnp.zeros_like(high_ref)
        normed_ref[:, reach + rows :] = jnp.zeros((blocks, reach, cols, LANES), jnp.float32)
        inv_ref[reach + rows :] = jnp.zeros((reach, cols, LANES), jnp.float32)

    text = text_ref[...]
    text_norm = jnp.sqrt(jnp.sum(text * text, axis=1, keepdims=True))
    unit_txt = text / text_norm
    txts_ref[me] = unit_txt
    txt_copies = exchange(
        "dp", lambda p: txts_ref.at[me], lambda j: txts_ref.at[me], sems[2], sems[3]
    )
    clear_edges(pad_ref, cols)
    clear_edges(gpad_ref, cols)

    def forward(b, carry):
        fill_taps(taps_ref, k_ref[:, lanes_of(b)])

        @pl.when(has_low)
        def _():
            to_high(b).wait_recv()

        @pl.when(has_high)
        def _():
            to_low(b).wait_recv()

        fill_padded(pad_ref, (low_ref[b], image_ref[:, :, lanes_of(b)], high_ref[b]), cols)
        bias = bias_ref[:, lanes_of(b)]
        for start in range(0, cols, TILE):
            acc = convolve(pad_ref, taps_ref, side, rows, start, False)
            for h in range(rows):
                normed_ref[b, reach + h, start : start + TILE, :] = (
                    acc[h].reshape(TILE, LANES) + bias
                )
        return carry

    lax.fori_loop(0, blocks, forward, 0)

    weight_ref[...] = jnp.zeros_like(weight_ref)

    def normalize(h, carry):
        r = reach + h
        total = normed_ref[0, r]
        for b in range(1, blocks):
            total = total + normed_ref[b, r]
        mu = jnp.sum(total, axis=1, keepdims=True) / channels
        mu = jnp.broadcast_to(mu, (cols, LANES))
        total = None
        for b in range(blocks):
            centred = normed_ref[b, r] - mu
            total = centred * centred if total is None else total + centred * centred
        spread = jnp.sum(total, axis=1, keepdims=True) / channels
        inv = jnp.broadcast_to(lax.rsqrt(spread + 1e-6), (cols, LANES))
        inv_ref[r] = inv
        for b in range(blocks):
            normed = (normed_ref[b, r] - mu) * inv
            normed_ref[b, r] = normed
            weight_ref[b] += jnp.sum(normed.reshape(cols // 8, 8, LANES), axis=0)
        return carry

    lax.fori_loop(0, rows, normalize, 0)
    for b in range(blocks):
        span = slice(b * LANES, (b + 1) * LANES)
        pool_ref[:, span] = (
            jnp.sum(weight_ref[b], axis=0, keepdims=True) * gain_ref[:, span]
            + (rows * cols) * shift_ref[:, span]
        )
    pool_copies = exchange("space", lambda p: pool_ref, lambda j: pools_ref.at[j], sems[0], sems[1])

    def wide(up):
        copies = []
        for i, ref in enumerate((normed_ref, inv_ref)):
            cut = (lambda a, z: ref.at[:, a:z]) if i == 0 else (lambda a, z: ref.at[a:z])
            source = cut(rows, rows + reach) if up else cut(reach, 2 * reach)
            target = cut(0, reach) if up else cut(rows + reach, rows + 2 * reach)
            copies.append(pltpu.make_async_remote_copy(
                src_ref=source, dst_ref=target,
                send_sem=wide_sems.at[0 if up else 2, i], recv_sem=wide_sems.at[1 if up else 3, i],
                device_id={"space": mine + 1 if up else mine - 1}, device_id_type=MESH,
            ))
        return copies

    @pl.when(has_high)
    def _():
        for copy in wide(True):
            copy.start()

    @pl.when(has_low)
    def _():
        for copy in wide(False):
            copy.start()

    proj_copy.wait()
    wait_all(pool_copies)
    pools_ref[0] = pool_ref[...]
    pooled = None
    for s in range(space):
        term = pools_ref[lax.rem(mine - s + space, space)]
        pooled = term if pooled is None else pooled + term
    pooled = pooled / pixel_count
    embedded = jnp.sum(
        jnp.dot(split3(pooled), proj_ref[...], preferred_element_type=jnp.float32),
        axis=0, keepdims=True,
    )
    emb_norm = jnp.sqrt(jnp.sum(embedded * embedded, axis=1, keepdims=True))
    unit_img = embedded / emb_norm
    imgs_ref[me] = unit_img
    img_copies = exchange(
        "dp", lambda p: imgs_ref.at[me], lambda j: imgs_ref.at[me], sems[4], sems[5]
    )
    wait_all(txt_copies)
    wait_all(img_copies)
    imgs = jnp.concatenate([imgs_ref[i] for i in range(dp)], axis=0)
    txts = jnp.concatenate([txts_ref[i] for i in range(dp)], axis=0)
    factor = scale_ref[0]
    row_id = lax.broadcasted_iota(jnp.int32, (dp, dp), 0)
    col_id = lax.broadcasted_iota(jnp.int32, (dp, dp), 1)
    scores = jnp.zeros((dp, dp), jnp.float32)
    turned = jnp.zeros((dp, dp), jnp.float32)
    for i in range(dp):
        column = factor * jnp.sum(imgs * txts[i : i + 1], axis=1, keepdims=True)
        scores = jnp.where(col_id == i, column, scores)
        column = factor * jnp.sum(txts * imgs[i : i + 1], axis=1, keepdims=True)
        turned = jnp.where(col_id == i, column, turned)
    identity = (row_id == col_id).astype(jnp.float32)
    row_ls, col_ls = logsum(scores, 1), logsum(scores, 0)
    trow_ls, tcol_ls = logsum(turned, 1), logsum(turned, 0)
    diagonal = jnp.sum(scores * identity, axis=1, keepdims=True)
    tdiagonal = jnp.sum(turned * identity, axis=1, keepdims=True)
    loss = jnp.sum(row_ls - diagonal, axis=0, keepdims=True) + jnp.sum(
        trow_ls - tdiagonal, axis=0, keepdims=True
    )
    loss_ref[...] = loss / (2 * dp)
    grad = 0.5 * (jnp.exp(scores - row_ls) + jnp.exp(scores - col_ls)) - identity
    tgrad = 0.5 * (jnp.exp(turned - trow_ls) + jnp.exp(turned - tcol_ls)) - identity
    own = (col_id == me).astype(jnp.float32)
    own_img = jnp.sum(tgrad * own, axis=1, keepdims=True)
    own_txt = jnp.sum(grad * own, axis=1, keepdims=True)
    unit_img_grad = factor * jnp.sum(own_img * txts, axis=0, keepdims=True)
    unit_txt_grad = factor * jnp.sum(own_txt * imgs, axis=0, keepdims=True)
    text_grad_ref[...] = (
        unit_txt_grad - unit_txt * jnp.sum(unit_txt * unit_txt_grad, axis=1, keepdims=True)
    ) / text_norm
    emb_grad = (
        unit_img_grad - unit_img * jnp.sum(unit_img * unit_img_grad, axis=1, keepdims=True)
    ) / emb_norm
    back = lax.dot_general(
        split3(emb_grad), proj_ref[...], (((1,), (1,)), ((), ())),
        preferred_element_type=jnp.float32,
    )
    weighted = jnp.sum(back, axis=0, keepdims=True) * gain_ref[...]
    weight_mean = jnp.sum(weighted, axis=1, keepdims=True) / channels
    for b in range(blocks):
        row = weighted[:, b * LANES : (b + 1) * LANES]
        weight_ref[b] = jnp.broadcast_to(row, (8, LANES))
        centred_ref[b] = jnp.broadcast_to(row - weight_mean, (8, LANES))

    def fill_coef(r, carry):
        total = None
        for b in range(blocks):
            term = normed_ref[b, r].reshape(cols // 8, 8, LANES) * weight_ref[b][None]
            total = term if total is None else total + term
        mean = jnp.sum(total.reshape(cols, LANES), axis=1, keepdims=True) / channels
        coef_ref[r] = inv_ref[r] * jnp.broadcast_to(mean, (cols, LANES))
        return carry

    def fill_grad(b, first, last):
        for r in range(first, last):
            base = (inv_ref[r].reshape(cols // 8, 8, LANES) * centred_ref[b][None]).reshape(
                cols, LANES
            )
            gpad_ref[r, PAD : PAD + cols, :] = base - normed_ref[b, r] * coef_ref[r]

    lax.fori_loop(reach, reach + rows, fill_coef, 0)
    part_ref[...] = jnp.zeros_like(part_ref)

    def kernel_terms(b, carry):
        fill_padded(pad_ref, (low_ref[b], image_ref[:, :, lanes_of(b)], high_ref[b]), cols)
        fill_grad(b, reach, reach + rows)
        for d in range(side):
            acc = [None] * side
            for w in range(0, cols, 8):
                own = [gpad_ref[reach + h, PAD + w : PAD + w + 8, :] for h in range(rows)]
                for r in range(rows + side - 1):
                    x = pad_ref[r, PAD - reach + d + w : PAD - reach + d + w + 8, :]
                    for a in range(side):
                        h = r - a
                        if 0 <= h < rows:
                            product = x * own[h]
                            acc[a] = product if acc[a] is None else acc[a] + product
            for a in range(side):
                part_ref[b // share, b % share, a, d : d + 1, :] = jnp.sum(
                    acc[a], axis=0, keepdims=True
                )
        return carry

    lax.fori_loop(0, blocks, kernel_terms, 0)

    def share_dp():
        return swap("dp", lambda p: part_ref.at[p], lambda j: dp_ref.at[j], sems[6], sems[7])

    def share_space():
        return swap("space", lambda p: mine_ref.at[:, pl.ds(p * owned, owned)],
                    lambda j: space_ref.at[j], sems[8], sems[9])

    def own_piece():
        return sum_ref.at[me, :, pl.ds(mine * owned, owned)]

    def back_space():
        return swap("space", lambda p: own_piece(), lambda j: own_piece(), sems[10], sems[11])

    def back_dp():
        return swap("dp", lambda p: sum_ref.at[me], lambda j: sum_ref.at[me], sems[12], sems[13])

    start_all(share_dp())

    @pl.when(has_high)
    def _():
        for copy in wide(True):
            copy.wait_send()
        for copy in wide(False):
            copy.wait_recv()

    @pl.when(has_low)
    def _():
        for copy in wide(False):
            copy.wait_send()
        for copy in wide(True):
            copy.wait_recv()

    lax.fori_loop(0, reach, fill_coef, 0)
    lax.fori_loop(reach + rows, rows + 2 * reach, fill_coef, 0)

    def input_grad(b, carry):
        @pl.when(b == blocks // 4)
        def _():
            wait_all(share_dp())
            total = part_ref[me]
            for j in range(1, dp):
                total = total + dp_ref[j]
            mine_ref[...] = total
            start_all(share_space())

        @pl.when(b == blocks // 2)
        def _():
            wait_all(share_space())
            total = mine_ref[:, pl.ds(mine * owned, owned)]
            for j in range(1, space):
                total = total + space_ref[j]
            sum_ref[me, :, pl.ds(mine * owned, owned)] = total / pixel_count
            start_all(back_space())

        @pl.when(b == 3 * blocks // 4)
        def _():
            wait_all(back_space())
            start_all(back_dp())

        fill_taps(taps_ref, k_ref[:, lanes_of(b)])
        fill_grad(b, 0, rows + 2 * reach)
        for start in range(0, cols, TILE):
            acc = convolve(gpad_ref, taps_ref, side, rows, start, True)
            for h in range(rows):
                grad_ref[h, start : start + TILE, lanes_of(b)] = (
                    acc[h].reshape(TILE, LANES).astype(grad_ref.dtype)
                )
        return carry

    lax.fori_loop(0, blocks, input_grad, 0)
    wait_all(back_dp())

    def image_sent(b, carry):
        @pl.when(has_high)
        def _():
            to_high(b).wait_send()

        @pl.when(has_low)
        def _():
            to_low(b).wait_send()

        return carry

    lax.fori_loop(0, blocks, image_sent, 0)


def shards(images, dw_kernel, dw_bias, ln_gain, ln_shift, proj, text, logit_scale):
    f32 = jnp.float32
    _, rows, cols, channels = images.shape
    side = dw_kernel.shape[0]
    reach = side // 2
    taps = side * side
    blocks = channels // LANES
    embed = proj.shape[1]
    dp, space = lax.axis_size("dp"), lax.axis_size("space")
    tall = rows + 2 * reach
    share = -(-blocks // dp)
    owned = -(-side // space)
    parts = (dp, share, space * owned, side, LANES)
    vmem = pl.BlockSpec(memory_space=pltpu.VMEM)
    dma = pltpu.SemaphoreType.DMA
    scratch = [
        pltpu.VMEM((blocks, reach, cols, LANES), jnp.bfloat16),
        pltpu.VMEM((blocks, reach, cols, LANES), jnp.bfloat16),
        pltpu.VMEM((blocks, tall, cols, LANES), f32),
        pltpu.VMEM((tall, cols, LANES), f32),
        pltpu.VMEM((tall, cols, LANES), f32),
        pltpu.VMEM((tall, cols + 2 * PAD, LANES), f32),
        pltpu.VMEM((tall, cols + 2 * PAD, LANES), f32),
        pltpu.VMEM((taps, 8, LANES), f32),
        pltpu.VMEM((1, channels), f32),
        pltpu.VMEM((blocks, 8, LANES), f32),
        pltpu.VMEM((blocks, 8, LANES), f32),
        pltpu.VMEM(proj.shape, proj.dtype),
        pltpu.VMEM((space, 1, channels), f32),
        pltpu.VMEM((dp, 1, embed), f32),
        pltpu.VMEM((dp, 1, embed), f32),
        pltpu.VMEM(parts, f32),
        pltpu.VMEM(parts, f32),
        pltpu.VMEM(parts[1:], f32),
        pltpu.VMEM((space, share, owned, side, LANES), f32),
        dma(()),
        dma((4, blocks)),
        dma((4, 2)),
    ]
    for size in (space, dp, dp, dp, space, space, dp):
        scratch += [dma((size,)), dma((size,))]
    grad_images, summed, loss, text_grad = pl.pallas_call(
        functools.partial(block_kernel, side, rows * space * cols),
        in_specs=[vmem] * 5 + [pl.BlockSpec(memory_space=pl.ANY), vmem,
                               pl.BlockSpec(memory_space=pltpu.SMEM)],
        out_specs=[vmem] * 4,
        out_shape=[
            jax.ShapeDtypeStruct((rows, cols, channels), jnp.bfloat16),
            jax.ShapeDtypeStruct(parts, f32),
            jax.ShapeDtypeStruct((1, 1), f32),
            jax.ShapeDtypeStruct((1, embed), f32),
        ],
        scratch_shapes=scratch,
        compiler_params=pltpu.CompilerParams(
            collective_id=0, has_side_effects=True, vmem_limit_bytes=VMEM_LIMIT
        ),
        name="block",
    )(images[0], dw_kernel.astype(f32).reshape(taps, channels), dw_bias.reshape(1, channels),
      ln_gain.reshape(1, channels), ln_shift.reshape(1, channels), proj, text, logit_scale)
    summed = summed.reshape(dp * share, space * owned, side, LANES)[:blocks, :side]
    kernel_grad = jnp.transpose(summed, (1, 2, 0, 3)).reshape(side, side, channels)
    return loss.reshape(()), grad_images[None], kernel_grad, text_grad


def solution(mesh):
    placed = (P("dp", "space", None, None), P(), P(), P(), P(), P(), P("dp", None), P())
    return jax.shard_map(
        shards,
        mesh=mesh,
        in_specs=placed,
        out_specs=(P(), P("dp", "space", None, None), P(), P("dp", None)),
        check_vma=False,
    )
```

time: 120 us -> 73.6 us (0.61)
  starting transfers between devices: 22.3 us -> 0 us
  Pallas kernels: 84 us -> 62.5 us
  waiting for transfers between devices: 1.64 us -> 0 us
    ppermute x6 -> x0, starting transfers between devices: 22.3 us -> none  [the longest x3 18.5 us: neighbours(): lax.ppermute(low_part, 'space', forward)]
    pallas_call x4 -> x1, Pallas kernels: 84 us -> 62.5 us  [shards(): pl.pallas_call(functools.partial(block_kernel, side, rows * space * cols)...]
    slice x3 -> x0, local copies, waits for them, and re-layouts: 6.04 us -> none  [the longest x1 3.54 us: shards(): nlow, nhigh = neighbours(normed[:, rows - reach:], normed[:, :reach])]
    unnamed x19 -> x6, local copies, waits for them, and re-layouts: 0.64 us -> 3.83 us
    reshape x3, local copies, waits for them, and re-layouts: 0.08 us -> 2.42 us  [the longest x1 0.97 us: shards(): dw_kernel.astype(f32).reshape(taps, channels)]
    ppermute x6 -> x0, waiting for transfers between devices: 1.64 us -> none  [the longest x3 1.63 us: neighbours(): lax.ppermute(low_part, 'space', forward)]
  transfers between devices with their start and end apart: 6 -> 0, of which waited for: 1 -> 0; matrix products, arithmetic and copies ran while one was open for 1% -> 0% of each run, Pallas kernels for 15% -> 0%
where the time goes in v2:
time: 73.6 us; the launch traced here: 73.2 us
  Pallas kernels  62.5 us (85%)
  local copies, waits for them, and re-layouts  7.65 us (10%)
  between operations  3.07 us (4%)
    pallas_call x1, Pallas kernels, shards(): pl.pallas_call(functools.partial(block_kernel, side, rows * space * cols)...  62.5 us
    unnamed x6, local copies, waits for them, and re-layouts  3.83 us

profile of v2, /device:TPU:0, one launch (start us, length us, event | category | flops | bytes accessed | tf_op | source)
XLA Modules:
  0.0 73.2 jit_solution(3445735584336886575)
XLA Ops:
  1.3 0.7 reshape.33.bias_ref
  2.0 0.7 reshape.34.gain_ref
  2.7 0.7 reshape.35.shift_ref
  3.4 1.0 %reshape.40.k_ref = f32[49,1536]{1,0:T(8,128)S(1)} reshape(bf16[7,7,1536]{2,1,0:T(8,128)(2,1)} %param.9) | data formatting | bytes 451584 | tf_op jit(solution)/shard_map/reshape | solution.py:512
  4.4 0.0 copy-start
  4.4 1.4 %copy-done = bf16[1,8,64,1536]{3,2,1,0:T(8,128)(2,1)S(1)} copy-done((bf16[1,8,64,1536]{3,2,1,0:T(8,128)(2,1)S(1)}, bf16[1,8,64,1536]{3,2,1,0:T(8,128)(2,1)}, u32[]{:S(2)}) %copy-start) | copy-done | bytes 1572888
  5.8 0.0 copy-start.1
  5.8 0.7 copy-done.1
  6.5 62.5 %block.1 = (bf16[8,64,1536]{2,1,0:T(8,128)(2,1)S(1)}, f32[4,3,8,7,128]{4,3,2,1,0:T(8,128)S(1)}, f32[1,1]{1,0:T(1,128)}, f32[1,1024]{1,0:T(1,128)S(1)}) custom-call(bf16[8,64,1536]{2,1,0:T(8,128)(2,1)S(1)} %bitcast.9, f32[49,1536]{1,0:T(8,128)S(1)} %reshape.40.k_ref, f32[1,1536]{1,0:T(1,128)S(1)} %reshape.33.bias_ref, f32[1,1536]{1,0:T(1,128)S(1)} %reshape.34.gain_ref, ...), custom_call_target="tpu_custom_call" | custom-call | tf_op jit(solution)/shard_map/block/pallas_call | solution.py:496
  69.0 0.8 %copy_bitcast_fusion = f32[7,7,1536]{2,1,0:T(8,128)} fusion(f32[12,8,7,128]{3,2,1,0:T(8,128)S(1)} %bitcast.10), kind=kLoop, calls=%fused_computation | loop fusion | bytes 645120 | tf_op jit(solution)/shard_map/reshape | solution.py:515
  70.4 1.1 %copy.21 = bf16[1,8,64,1536]{3,2,1,0:T(8,128)(2,1)} copy(bf16[1,8,64,1536]{3,2,1,0:T(8,128)(2,1)S(1)} %bitcast.8) | data formatting | bytes 3145728
  71.5 0.6 copy.22
Async XLA Ops:
  4.4 1.4 %copy-start = (bf16[1,8,64,1536]{3,2,1,0:T(8,128)(2,1)S(1)}, bf16[1,8,64,1536]{3,2,1,0:T(8,128)(2,1)}, u32[]{:S(2)}) copy-start(bf16[1,8,64,1536]{3,2,1,0:T(8,128)(2,1)} %param.8) | copy-start | bytes 4718596
  5.8 0.7 copy-start.1

commit v3 on v2

--- a/solution.py
+++ b/solution.py
@@ -10,13 +10,16 @@
 LANES = 128
 PAD = 8
 TILE = 32
-VMEM_LIMIT = 50 * 1024 * 1024
+VMEM_LIMIT = 63 * 1024 * 1024
 MESH = pl.DeviceIdType.MESH
 
 
-def fill_taps(taps_ref, rows):
-    for i in range(rows.shape[0]):
-        taps_ref[i] = jnp.broadcast_to(rows[i : i + 1, :], taps_ref.shape[1:])
+def fill_taps(taps_ref, k_ref, lanes):
+    side = k_ref.shape[0]
+    for a in range(side):
+        rows = k_ref[a, :, lanes].astype(jnp.float32)
+        for d in range(side):
+            taps_ref[a * side + d] = jnp.broadcast_to(rows[d : d + 1, :], taps_ref.shape[1:])
 
 
 def fill_padded(pad_ref, parts, cols):
@@ -116,13 +119,13 @@
 
 
 def block_kernel(side, pixel_count,
-                 image_ref, k_ref, bias_ref, gain_ref, shift_ref, proj_hbm, text_ref, scale_ref,
+                 image_hbm, k_hbm, bias_hbm, gain_hbm, shift_hbm, proj_hbm, text_hbm, scale_ref,
                  grad_ref, sum_ref, loss_ref, text_grad_ref,
-                 low_ref, high_ref, normed_ref, inv_ref, coef_ref, pad_ref, gpad_ref, taps_ref,
+                 image_ref, k_ref, bias_ref, gain_ref, shift_ref, text_ref, low_ref, high_ref, normed_ref, inv_ref, coef_ref, pad_ref, gpad_ref, taps_ref,
                  pool_ref, weight_ref, centred_ref, proj_ref, pools_ref, txts_ref, imgs_ref,
                  part_ref, dp_ref, mine_ref, space_ref,
-                 proj_sem, image_sems, wide_sems, *sems):
-    rows, cols, channels = image_ref.shape
+                 local_sems, image_sems, wide_sems, *sems):
+    rows, cols, channels = image_hbm.shape
     blocks = channels // LANES
     reach = side // 2
     dp, space = lax.axis_size("dp"), lax.axis_size("space")
@@ -130,20 +133,26 @@
     has_low, has_high = mine > 0, mine < space - 1
     share, owned = part_ref.shape[1], part_ref.shape[2] // space
 
-    proj_copy = pltpu.make_async_copy(proj_hbm, proj_ref, proj_sem)
-    proj_copy.start()
+    image_copy = pltpu.make_async_copy(image_hbm, image_ref, local_sems.at[0])
+    bias_copy = pltpu.make_async_copy(bias_hbm, bias_ref.at[0], local_sems.at[1])
+    gain_copy = pltpu.make_async_copy(gain_hbm, gain_ref.at[0], local_sems.at[2])
+    shift_copy = pltpu.make_async_copy(shift_hbm, shift_ref.at[0], local_sems.at[3])
+    proj_copy = pltpu.make_async_copy(proj_hbm, proj_ref, local_sems.at[4])
+    text_copy = pltpu.make_async_copy(text_hbm, text_ref, local_sems.at[5])
+    k_copy = pltpu.make_async_copy(k_hbm, k_ref, local_sems.at[6])
+    start_all([text_copy, image_copy, k_copy, bias_copy, gain_copy, shift_copy, proj_copy])
     entry_barrier(("dp", "space"))
 
     def to_high(b):
         return pltpu.make_async_remote_copy(
-            src_ref=image_ref.at[rows - reach : rows, :, lanes_of(b)], dst_ref=low_ref.at[b],
+            src_ref=image_hbm.at[rows - reach : rows, :, lanes_of(b)], dst_ref=low_ref.at[b],
             send_sem=image_sems.at[0, b], recv_sem=image_sems.at[1, b],
             device_id={"space": mine + 1}, device_id_type=MESH,
         )
 
     def to_low(b):
         return pltpu.make_async_remote_copy(
-            src_ref=image_ref.at[0:reach, :, lanes_of(b)], dst_ref=high_ref.at[b],
+            src_ref=image_hbm.at[0:reach, :, lanes_of(b)], dst_ref=high_ref.at[b],
             send_sem=image_sems.at[2, b], recv_sem=image_sems.at[3, b],
             device_id={"space": mine - 1}, device_id_type=MESH,
         )
@@ -173,6 +182,7 @@
         normed_ref[:, reach + rows :] = jnp.zeros((blocks, reach, cols, LANES), jnp.float32)
         inv_ref[reach + rows :] = jnp.zeros((reach, cols, LANES), jnp.float32)
 
+    text_copy.wait()
     text = text_ref[...]
     text_norm = jnp.sqrt(jnp.sum(text * text, axis=1, keepdims=True))
     unit_txt = text / text_norm
@@ -182,9 +192,10 @@
     )
     clear_edges(pad_ref, cols)
     clear_edges(gpad_ref, cols)
+    wait_all([image_copy, k_copy, bias_copy, gain_copy, shift_copy])
 
     def forward(b, carry):
-        fill_taps(taps_ref, k_ref[:, lanes_of(b)])
+        fill_taps(taps_ref, k_ref, lanes_of(b))
 
         @pl.when(has_low)
         def _():
@@ -250,6 +261,9 @@
             ))
         return copies
 
+    proj_copy.wait()
+    wait_all(pool_copies)
+
     @pl.when(has_high)
     def _():
         for copy in wide(True):
@@ -260,8 +274,6 @@
         for copy in wide(False):
             copy.start()
 
-    proj_copy.wait()
-    wait_all(pool_copies)
     pools_ref[0] = pool_ref[...]
     pooled = None
     for s in range(space):
@@ -425,7 +437,7 @@
             wait_all(back_space())
             start_all(back_dp())
 
-        fill_taps(taps_ref, k_ref[:, lanes_of(b)])
+        fill_taps(taps_ref, k_ref, lanes_of(b))
         fill_grad(b, 0, rows + 2 * reach)
         for start in range(0, cols, TILE):
             acc = convolve(gpad_ref, taps_ref, side, rows, start, True)
@@ -466,8 +478,15 @@
     owned = -(-side // space)
     parts = (dp, share, space * owned, side, LANES)
     vmem = pl.BlockSpec(memory_space=pltpu.VMEM)
+    hbm = pl.BlockSpec(memory_space=pltpu.HBM)
     dma = pltpu.SemaphoreType.DMA
     scratch = [
+        pltpu.VMEM((rows, cols, channels), jnp.bfloat16),
+        pltpu.VMEM(dw_kernel.shape, dw_kernel.dtype),
+        pltpu.VMEM((1, channels), f32),
+        pltpu.VMEM((1, channels), f32),
+        pltpu.VMEM((1, channels), f32),
+        pltpu.VMEM((1, embed), f32),
         pltpu.VMEM((blocks, reach, cols, LANES), jnp.bfloat16),
         pltpu.VMEM((blocks, reach, cols, LANES), jnp.bfloat16),
         pltpu.VMEM((blocks, tall, cols, LANES), f32),
@@ -487,7 +506,7 @@
         pltpu.VMEM(parts, f32),
         pltpu.VMEM(parts[1:], f32),
         pltpu.VMEM((space, share, owned, side, LANES), f32),
-        dma(()),
+        dma((7,)),
         dma((4, blocks)),
         dma((4, 2)),
     ]
@@ -495,7 +514,7 @@
         scratch += [dma((size,)), dma((size,))]
     grad_images, summed, loss, text_grad = pl.pallas_call(
         functools.partial(block_kernel, side, rows * space * cols),
-        in_specs=[vmem] * 5 + [pl.BlockSpec(memory_space=pl.ANY), vmem,
+        in_specs=[hbm] * 7 + [
                                pl.BlockSpec(memory_space=pltpu.SMEM)],
         out_specs=[vmem] * 4,
         out_shape=[
@@ -509,8 +528,7 @@
             collective_id=0, has_side_effects=True, vmem_limit_bytes=VMEM_LIMIT
         ),
         name="block",
-    )(images[0], dw_kernel.astype(f32).reshape(taps, channels), dw_bias.reshape(1, channels),
-      ln_gain.reshape(1, channels), ln_shift.reshape(1, channels), proj, text, logit_scale)
+    )(images[0], dw_kernel, dw_bias, ln_gain, ln_shift, proj, text, logit_scale)
     summed = summed.reshape(dp * share, space * owned, side, LANES)[:blocks, :side]
     kernel_grad = jnp.transpose(summed, (1, 2, 0, 3)).reshape(side, side, channels)
     return loss.reshape(()), grad_images[None], kernel_grad, text_grad

time: 73.6 us -> 71.6 us (0.973)
  local copies, waits for them, and re-layouts: 7.65 us -> 4.99 us
  Pallas kernels: 62.5 us -> 63.4 us
    reshape x4 -> x0, local copies, waits for them, and re-layouts: 3.07 us -> none  [the longest x1 0.97 us: shards(): dw_kernel.astype(f32).reshape(taps, channels)]
    reshape x1, local copies, waits for them, and re-layouts: 0.75 us -> 1.74 us  [shards(): jnp.transpose(summed, (1, 2, 0, 3)).reshape(side, side, channels)]
    pallas_call x1, Pallas kernels: 62.5 us -> 63.4 us  [shards(): pl.pallas_call(functools.partial(block_kernel, side, rows * space * cols)...]
    unnamed x6 -> x4, local copies, waits for them, and re-layouts: 3.83 us -> 3.25 us
where the time goes in v3:
time: 71.6 us; the launch traced here: 71.4 us
  Pallas kernels  63.4 us (89%)
  local copies, waits for them, and re-layouts  4.99 us (7%)
  between operations  3.07 us (4%)
    pallas_call x1, Pallas kernels, shards(): pl.pallas_call(functools.partial(block_kernel, side, rows * space * cols)...  63.4 us
    unnamed x4, local copies, waits for them, and re-layouts  3.25 us
    reshape x1, local copies, waits for them, and re-layouts, shards(): jnp.transpose(summed, (1, 2, 0, 3)).reshape(side, side, channels)  1.74 us

profile of v3, /device:TPU:0, one launch (start us, length us, event | category | flops | bytes accessed | tf_op | source)
XLA Modules:
  0.0 71.4 jit_solution(13621207347662393901)
XLA Ops:
  1.3 63.4 %block.1 = (bf16[8,64,1536]{2,1,0:T(8,128)(2,1)}, f32[4,3,8,7,128]{4,3,2,1,0:T(8,128)}, f32[1,1]{1,0:T(1,128)}, f32[1,1024]{1,0:T(1,128)}) custom-call(bf16[8,64,1536]{2,1,0:T(8,128)(2,1)} %bitcast.9, bf16[7,7,1536]{2,1,0:T(8,128)(2,1)} %k_hbm.1, f32[1536]{0:T(1024)} %bias_hbm.1, f32[1536]{0:T(1024)} %gain_hbm.1, f32[1536]{0:T(1024)} %shift_hbm.1, ...), custom_call_target="tpu_custom_call" | custom-call | tf_op jit(solution)/shard_map/block/pallas_call | solution.py:515
  64.7 1.7 %copy_bitcast_fusion = f32[7,7,1536]{2,1,0:T(8,128)} fusion(f32[12,8,7,128]{3,2,1,0:T(8,128)} %bitcast.10), kind=kLoop, calls=%fused_computation | loop fusion | bytes 645120 | tf_op jit(solution)/shard_map/reshape | solution.py:533
  67.0 0.0 copy-start
  67.0 2.7 %copy.21 = bf16[1,8,64,1536]{3,2,1,0:T(8,128)(2,1)} copy(bf16[1,8,64,1536]{3,2,1,0:T(8,128)(2,1)} %bitcast.8) | data formatting | bytes 3145728
  69.7 0.0 copy-done
  69.7 0.6 copy.22
Async XLA Ops:
  67.0 2.7 %copy-start = (f32[1,1024]{1,0:T(1,128)S(1)}, f32[1,1024]{1,0:T(1,128)}, u32[]{:S(2)}) copy-start(f32[1,1024]{1,0:T(1,128)} %get-tuple-element.19) | copy-start | bytes 12292

commit v4 on v3

--- a/solution.py
+++ b/solution.py
@@ -122,7 +122,7 @@
                  image_hbm, k_hbm, bias_hbm, gain_hbm, shift_hbm, proj_hbm, text_hbm, scale_ref,
                  grad_ref, sum_ref, loss_ref, text_grad_ref,
                  image_ref, k_ref, bias_ref, gain_ref, shift_ref, text_ref, low_ref, high_ref, normed_ref, inv_ref, coef_ref, pad_ref, gpad_ref, taps_ref,
-                 pool_ref, weight_ref, centred_ref, proj_ref, pools_ref, txts_ref, imgs_ref,
+                 pool_ref, weight_ref, centred_ref, proj_ref, turned_ref, pools_ref, txts_ref, imgs_ref,
                  part_ref, dp_ref, mine_ref, space_ref,
                  local_sems, image_sems, wide_sems, *sems):
     rows, cols, channels = image_hbm.shape
@@ -192,6 +192,10 @@
     )
     clear_edges(pad_ref, cols)
     clear_edges(gpad_ref, cols)
+    proj_copy.wait()
+    for b in range(blocks):
+        span = slice(b * LANES, (b + 1) * LANES)
+        turned_ref[:, span] = proj_ref[span, :].T
     wait_all([image_copy, k_copy, bias_copy, gain_copy, shift_copy])
 
     def forward(b, carry):
@@ -261,7 +265,6 @@
             ))
         return copies
 
-    proj_copy.wait()
     wait_all(pool_copies)
 
     @pl.when(has_high)
@@ -326,10 +329,7 @@
     emb_grad = (
         unit_img_grad - unit_img * jnp.sum(unit_img * unit_img_grad, axis=1, keepdims=True)
     ) / emb_norm
-    back = lax.dot_general(
-        split3(emb_grad), proj_ref[...], (((1,), (1,)), ((), ())),
-        preferred_element_type=jnp.float32,
-    )
+    back = jnp.dot(split3(emb_grad), turned_ref[...], preferred_element_type=jnp.float32)
     weighted = jnp.sum(back, axis=0, keepdims=True) * gain_ref[...]
     weight_mean = jnp.sum(weighted, axis=1, keepdims=True) / channels
     for b in range(blocks):
@@ -355,6 +355,16 @@
 
     lax.fori_loop(reach, reach + rows, fill_coef, 0)
     part_ref[...] = jnp.zeros_like(part_ref)
+
+    def piece(owner, k, j):
+        return pltpu.make_async_remote_copy(
+            src_ref=part_ref.at[owner, k], dst_ref=dp_ref.at[j, k],
+            send_sem=sems[6].at[j, k], recv_sem=sems[7].at[j, k],
+            device_id={"dp": owner}, device_id_type=MESH,
+        )
+
+    def to_owner(b):
+        return piece(b // share, b % share, lax.rem(b // share - me + dp, dp))
 
     def kernel_terms(b, carry):
         fill_padded(pad_ref, (low_ref[b], image_ref[:, :, lanes_of(b)], high_ref[b]), cols)
@@ -374,12 +384,14 @@
                 part_ref[b // share, b % share, a, d : d + 1, :] = jnp.sum(
                     acc[a], axis=0, keepdims=True
                 )
+
+        @pl.when(b // share != me)
+        def _():
+            to_owner(b).start()
+
         return carry
 
     lax.fori_loop(0, blocks, kernel_terms, 0)
-
-    def share_dp():
-        return swap("dp", lambda p: part_ref.at[p], lambda j: dp_ref.at[j], sems[6], sems[7])
 
     def share_space():
         return swap("space", lambda p: mine_ref.at[:, pl.ds(p * owned, owned)],
@@ -393,8 +405,6 @@
 
     def back_dp():
         return swap("dp", lambda p: sum_ref.at[me], lambda j: sum_ref.at[me], sems[12], sems[13])
-
-    start_all(share_dp())
 
     @pl.when(has_high)
     def _():
@@ -414,16 +424,20 @@
     lax.fori_loop(reach + rows, rows + 2 * reach, fill_coef, 0)
 
     def input_grad(b, carry):
-        @pl.when(b == blocks // 4)
-        def _():
-            wait_all(share_dp())
+        @pl.when(b == 1)
+        def _():
+            for j in range(1, dp):
+                for k in range(share):
+                    @pl.when(me * share + k < blocks)
+                    def _():
+                        piece(lax.rem(me + j, dp), k, j).wait_recv()
             total = part_ref[me]
             for j in range(1, dp):
                 total = total + dp_ref[j]
             mine_ref[...] = total
             start_all(share_space())
 
-        @pl.when(b == blocks // 2)
+        @pl.when(b == blocks // 3)
         def _():
             wait_all(share_space())
             total = mine_ref[:, pl.ds(mine * owned, owned)]
@@ -432,7 +446,7 @@
             sum_ref[me, :, pl.ds(mine * owned, owned)] = total / pixel_count
             start_all(back_space())
 
-        @pl.when(b == 3 * blocks // 4)
+        @pl.when(b == 7 * blocks // 12)
         def _():
             wait_all(back_space())
             start_all(back_dp())
@@ -451,6 +465,10 @@
     wait_all(back_dp())
 
     def image_sent(b, carry):
+        @pl.when(b // share != me)
+        def _():
+            to_owner(b).wait_send()
+
         @pl.when(has_high)
         def _():
             to_high(b).wait_send()
@@ -499,6 +517,7 @@
         pltpu.VMEM((blocks, 8, LANES), f32),
         pltpu.VMEM((blocks, 8, LANES), f32),
         pltpu.VMEM(proj.shape, proj.dtype),
+        pltpu.VMEM(proj.shape[::-1], proj.dtype),
         pltpu.VMEM((space, 1, channels), f32),
         pltpu.VMEM((dp, 1, embed), f32),
         pltpu.VMEM((dp, 1, embed), f32),
@@ -510,8 +529,8 @@
         dma((4, blocks)),
         dma((4, 2)),
     ]
-    for size in (space, dp, dp, dp, space, space, dp):
-        scratch += [dma((size,)), dma((size,))]
+    for shape in ((space,), (dp,), (dp,), (dp, share), (space,), (space,), (dp,)):
+        scratch += [dma(shape), dma(shape)]
     grad_images, summed, loss, text_grad = pl.pallas_call(
         functools.partial(block_kernel, side, rows * space * cols),
         in_specs=[hbm] * 7 + [

time: 71.6 us -> 69.3 us (0.968)
  Pallas kernels: 63.4 us -> 61 us
    pallas_call x1, Pallas kernels: 63.4 us -> 61 us  [shards(): pl.pallas_call(functools.partial(block_kernel, side, rows * space * cols)...]
where the time goes in v4:
time: 69.3 us; the launch traced here: 69.1 us
  Pallas kernels  61 us (88%)
  local copies, waits for them, and re-layouts  4.99 us (7%)
  between operations  3.07 us (4%)
    pallas_call x1, Pallas kernels, shards(): pl.pallas_call(functools.partial(block_kernel, side, rows * space * cols)...  61 us
    unnamed x4, local copies, waits for them, and re-layouts  3.25 us
    reshape x1, local copies, waits for them, and re-layouts, shards(): jnp.transpose(summed, (1, 2, 0, 3)).reshape(side, side, channels)  1.74 us

profile of v4, /device:TPU:0, one launch (start us, length us, event | category | flops | bytes accessed | tf_op | source)
XLA Modules:
  0.0 69.1 jit_solution(10696316531933528268)
XLA Ops:
  1.3 61.0 %block.1 = (bf16[8,64,1536]{2,1,0:T(8,128)(2,1)}, f32[4,3,8,7,128]{4,3,2,1,0:T(8,128)}, f32[1,1]{1,0:T(1,128)}, f32[1,1024]{1,0:T(1,128)}) custom-call(bf16[8,64,1536]{2,1,0:T(8,128)(2,1)} %bitcast.9, bf16[7,7,1536]{2,1,0:T(8,128)(2,1)} %k_hbm.1, f32[1536]{0:T(1024)} %bias_hbm.1, f32[1536]{0:T(1024)} %gain_hbm.1, f32[1536]{0:T(1024)} %shift_hbm.1, ...), custom_call_target="tpu_custom_call" | custom-call | tf_op jit(solution)/shard_map/block/pallas_call | solution.py:534
  62.3 1.7 %copy_bitcast_fusion = f32[7,7,1536]{2,1,0:T(8,128)} fusion(f32[12,8,7,128]{3,2,1,0:T(8,128)} %bitcast.10), kind=kLoop, calls=%fused_computation | loop fusion | bytes 645120 | tf_op jit(solution)/shard_map/reshape | solution.py:552
  64.7 0.0 copy-start
  64.7 2.7 %copy.21 = bf16[1,8,64,1536]{3,2,1,0:T(8,128)(2,1)} copy(bf16[1,8,64,1536]{3,2,1,0:T(8,128)(2,1)} %bitcast.8) | data formatting | bytes 3145728
  67.3 0.0 copy-done
  67.3 0.6 copy.22
Async XLA Ops:
  64.7 2.7 %copy-start = (f32[1,1024]{1,0:T(1,128)S(1)}, f32[1,1024]{1,0:T(1,128)}, u32[]{:S(2)}) copy-start(f32[1,1024]{1,0:T(1,128)} %get-tuple-element.19) | copy-start | bytes 12292

commit v5 on v4

--- a/solution.py
+++ b/solution.py
@@ -10,7 +10,7 @@
 LANES = 128
 PAD = 8
 TILE = 32
-VMEM_LIMIT = 63 * 1024 * 1024
+VMEM_LIMIT = 50 * 1024 * 1024
 MESH = pl.DeviceIdType.MESH
 
 

time: 69.3 us -> 71.5 us (1.032)
  local copies, waits for them, and re-layouts: 4.99 us -> 7.59 us
    unnamed x4 -> x14, local copies, waits for them, and re-layouts: 3.25 us -> 6.83 us
    reshape x1, local copies, waits for them, and re-layouts: 1.74 us -> 0.75 us  [shards(): jnp.transpose(summed, (1, 2, 0, 3)).reshape(side, side, channels)]
where the time goes in v5:
time: 71.5 us; the launch traced here: 71.1 us
  Pallas kernels  60.4 us (84%)
  local copies, waits for them, and re-layouts  7.59 us (11%)
  between operations  3.13 us (4%)
    pallas_call x1, Pallas kernels, shards(): pl.pallas_call(functools.partial(block_kernel, side, rows * space * cols)...  60.4 us
    unnamed x14, local copies, waits for them, and re-layouts  6.83 us

profile of v5, /device:TPU:0, one launch (start us, length us, event | category | flops | bytes accessed | tf_op | source)
XLA Modules:
  0.0 71.1 jit_solution(9638910148054463005)
XLA Ops:
  1.3 0.0 copy-start
  1.3 1.4 %copy-done = bf16[1,8,64,1536]{3,2,1,0:T(8,128)(2,1)S(1)} copy-done((bf16[1,8,64,1536]{3,2,1,0:T(8,128)(2,1)S(1)}, bf16[1,8,64,1536]{3,2,1,0:T(8,128)(2,1)}, u32[]{:S(2)}) %copy-start) | copy-done | bytes 1572888
  2.7 0.0 copy-start.1
  2.7 0.9 %copy-done.1 = bf16[7,7,1536]{2,1,0:T(8,128)(2,1)S(1)} copy-done((bf16[7,7,1536]{2,1,0:T(8,128)(2,1)S(1)}, bf16[7,7,1536]{2,1,0:T(8,128)(2,1)}, u32[]{:S(2)}) %copy-start.1) | copy-done | bytes 150552
  3.6 0.0 copy-start.2
  3.6 0.7 copy-done.2
  4.3 0.0 copy-start.3
  4.3 0.7 copy-done.3
  5.0 0.0 copy-start.4
  5.0 0.7 copy-done.4
  5.7 0.0 copy-start.5
  5.7 0.7 copy-done.5
  6.4 60.4 %block.1 = (bf16[8,64,1536]{2,1,0:T(8,128)(2,1)S(1)}, f32[4,3,8,7,128]{4,3,2,1,0:T(8,128)S(1)}, f32[1,1]{1,0:T(1,128)}, f32[1,1024]{1,0:T(1,128)S(1)}) custom-call(bf16[8,64,1536]{2,1,0:T(8,128)(2,1)S(1)} %bitcast.9, bf16[7,7,1536]{2,1,0:T(8,128)(2,1)S(1)} %copy-done.1, f32[1536]{0:T(1024)S(1)} %copy-done.2, f32[1536]{0:T(1024)S(1)} %copy-done.3, ...), custom_call_target="tpu_custom_call" | custom-call | tf_op jit(solution)/shard_map/block/pallas_call | solution.py:534
  66.8 0.8 %copy_bitcast_fusion = f32[7,7,1536]{2,1,0:T(8,128)} fusion(f32[12,8,7,128]{3,2,1,0:T(8,128)S(1)} %bitcast.10), kind=kLoop, calls=%fused_computation | loop fusion | bytes 645120 | tf_op jit(solution)/shard_map/reshape | solution.py:552
  68.2 1.1 %copy.21 = bf16[1,8,64,1536]{3,2,1,0:T(8,128)(2,1)} copy(bf16[1,8,64,1536]{3,2,1,0:T(8,128)(2,1)S(1)} %bitcast.8) | data formatting | bytes 3145728
  69.4 0.6 copy.22
Async XLA Ops:
  1.3 1.4 %copy-start = (bf16[1,8,64,1536]{3,2,1,0:T(8,128)(2,1)S(1)}, bf16[1,8,64,1536]{3,2,1,0:T(8,128)(2,1)}, u32[]{:S(2)}) copy-start(bf16[1,8,64,1536]{3,2,1,0:T(8,128)(2,1)} %param.8) | copy-start | bytes 4718596
  2.7 0.9 %copy-start.1 = (bf16[7,7,1536]{2,1,0:T(8,128)(2,1)S(1)}, bf16[7,7,1536]{2,1,0:T(8,128)(2,1)}, u32[]{:S(2)}) copy-start(bf16[7,7,1536]{2,1,0:T(8,128)(2,1)} %k_hbm.1) | copy-start | bytes 451588
  3.6 0.7 copy-start.2
  4.3 0.7 copy-start.3
  5.0 0.7 copy-start.4
  5.7 0.7 copy-start.5
